TPU v7x, 32 devices: a whole 2x2x4 slice. The times are simulated.
32 devices in a mesh: pairs: 16 (over z, y, x), aux: 2 (over core).
Axes of the slice: x: 2, y: 2, z: 4, core: 2. Of those that a mesh axis runs over, the one named last changes fastest.
Arguments:
- blocks: bfloat16 [32, 2048, 256], P('pairs', 'aux'), may hold values from -0.9 to 0.9
- pair_orbs: int32 [256, 2], P('pairs'), may hold values from 0 to 31, as said below
- pno_count: int32 [256], P('pairs'), may hold values from 128 to 256
- amplitudes: bfloat16 [256, 256, 256], P('pairs'), may hold values from -6 to 6
- margins: bfloat16 [256, 4, 256, 256], P('pairs'), may hold values from -0.375 to 0.375
- couple_target: int32 [256, 4], replicated, may hold values from 0 to 255, as said below
- couple_weight: float32 [256, 4], replicated, may hold values from -1 to 1
- pno_energy: float32 [256, 256], P('pairs'), may hold values from 0.3 to 4
- occ_energy: float32 [32], replicated, may hold values from -2 to -0.3
Outputs:
- residual: float32 [256, 256, 256], P('pairs', 'aux')
Inputs may be any that keep to these rules, and one draw needn't show every extreme that they name: `pair_orbs`: the first orbital of pair p belongs to pairs index p // 16 (orbitals o with o // 2 equal to it); the second belongs to that index or an adjacent one. `couple_target`: every target of source pair q is held by pairs index q // 16 or an adjacent one (target t is held by index t // 16).
All inputs are finite; a program needn't handle non-finite values.
Results may differ from a plain program's by a relative error of at most 0.00076.
Values may be sent and summed in bfloat16 or wider, within the bound.
A program may use at most 128 MiB of HBM per device.

v0:
```python
import jax
import jax.numpy as jnp
from jax import lax
from jax.sharding import PartitionSpec as P


def with_halo(cells, sides, width):
    for axis, dim in sides:
        count = lax.axis_size(axis)
        ends = count - 1
        head = lax.slice_in_dim(cells, 0, width, axis=dim)
        tail = lax.slice_in_dim(cells, cells.shape[dim] - width, cells.shape[dim], axis=dim)
        cells = jnp.concatenate(
            [
                lax.ppermute(tail, axis, [(i, (i + 1) % count) for i in range(ends)]),
                cells,
                lax.ppermute(head, axis, [((i + 1) % count, i) for i in range(ends)]),
            ],
            axis=dim,
        )
    return cells


def passed_along(value, axis, steps):
    count = lax.axis_size(axis)
    leading, last = (max(0, -steps), min(count, count - steps))
    return lax.ppermute(value, axis, [(source, source + steps) for source in range(leading, last)])


def coupling_terms(source_margins, source_amplitudes, weights, row_start, row_count):
    margin_rows = lax.dynamic_slice_in_dim(source_margins, row_start, row_count, 2)
    first_product = jnp.einsum(
        "pcak,pkl->pcal", margin_rows, source_amplitudes, preferred_element_type=jnp.float32
    ).astype(jnp.bfloat16)
    second = jnp.einsum(
        "pcal,pcbl->pcab", first_product, source_margins, preferred_element_type=jnp.float32
    )
    return second * weights[:, :, None, None]


def route_terms(pair_terms, local_slots, slot_total):
    flat_terms = pair_terms.reshape((-1,) + pair_terms.shape[2:])
    flat_slots = local_slots.reshape(-1)
    inside = (flat_slots >= 0) & (flat_slots < slot_total)
    flat_slots = jnp.where(inside, flat_slots, slot_total)
    empty = jnp.zeros((slot_total,) + pair_terms.shape[2:], jnp.float32)
    return empty.at[flat_slots].add(flat_terms, mode="drop")


def local(
    blocks,
    pair_orbs,
    pno_count,
    amplitudes,
    margins,
    couple_target,
    couple_weight,
    pno_energy,
    occ_energy,
):
    holder = lax.axis_index("pairs")
    core_index = lax.axis_index("aux")
    pair_count = amplitudes.shape[0]
    orb_count = blocks.shape[0]
    pno_width = amplitudes.shape[2]
    row_count = pno_width // lax.axis_size("aux")
    row_start = core_index * row_count
    padded = with_halo(blocks, (("pairs", 0),), orb_count)
    base_orb = (holder - 1) * orb_count
    left_block = padded[pair_orbs[:, 0] - base_orb]
    right_block = padded[pair_orbs[:, 1] - base_orb]
    partial_value = jnp.einsum(
        "pqa,pqb->pab", left_block, right_block, preferred_element_type=jnp.float32
    )
    summed = lax.psum(partial_value, "aux")
    exchange_rows = lax.dynamic_slice_in_dim(summed, row_start, row_count, 1)
    orbitals = jnp.arange(occ_energy.shape[0], dtype=jnp.int32)
    occ_first = jnp.sum(
        jnp.where(pair_orbs[:, 0:1] == orbitals[None, :], occ_energy[None, :], 0.0), axis=1
    )
    occ_second = jnp.sum(
        jnp.where(pair_orbs[:, 1:2] == orbitals[None, :], occ_energy[None, :], 0.0), axis=1
    )
    energy_rows = lax.dynamic_slice_in_dim(pno_energy, row_start, row_count, 1)
    amp_rows = lax.dynamic_slice_in_dim(amplitudes, row_start, row_count, 1).astype(jnp.float32)
    denominator = (
        energy_rows[:, :, None] + pno_energy[:, None, :] - (occ_first + occ_second)[:, None, None]
    )
    base_terms = exchange_rows + denominator * amp_rows
    own_targets = lax.dynamic_slice_in_dim(couple_target, holder * pair_count, pair_count, 0)
    own_weights = lax.dynamic_slice_in_dim(couple_weight, holder * pair_count, pair_count, 0)
    pair_terms = coupling_terms(margins, amplitudes, own_weights, row_start, row_count)
    local_slots = own_targets - (holder - 1) * pair_count
    grouped = route_terms(pair_terms, local_slots, 3 * pair_count)
    grouped = grouped.reshape((3, pair_count) + grouped.shape[1:])
    from_lower = passed_along(grouped[2], "pairs", 1)
    from_upper = passed_along(grouped[0], "pairs", -1)
    coupling = grouped[1] + from_lower + from_upper
    positions = jnp.arange(pno_width, dtype=jnp.int32)
    col_mask = (positions[None, :] < pno_count[:, None]).astype(jnp.float32)
    row_positions = row_start + jnp.arange(row_count, dtype=jnp.int32)
    row_mask = (row_positions[None, :] < pno_count[:, None]).astype(jnp.float32)
    return (base_terms + coupling) * row_mask[:, :, None] * col_mask[:, None, :]


def solution(mesh):
    placed = (
        P("pairs", "aux", None),
        P("pairs", None),
        P("pairs"),
        P("pairs", None, None),
        P("pairs", None, None, None),
        P(),
        P(),
        P("pairs", None),
        P(),
    )
    return jax.shard_map(
        local, mesh=mesh, in_specs=placed, out_specs=P("pairs", "aux", None), check_vma=False
    )
```

profile of v0, /device:TPU:12, one launch (start us, length us, event | category | flops | bytes accessed | tf_op | source)
XLA Modules:
  0.0 225.0 jit_solution(12098138309565955443)
XLA Ops:
  6.5 3.5 %collective-permute-start = (bf16[2,1024,256]{2,1,0:T(8,128)(2,1)}, bf16[2,1024,256]{2,1,0:T(8,128)(2,1)}, u32[]{:S(2)}, u32[]{:S(2)}) collective-permute-start(bf16[2,1024,256]{2,1,0:T(8,128)(2,1)} %param.9), channel_id=1, source_target_pairs={{0,2},{2,4},{4,6},{6,8},{8,10},{10,12},{12,14},{14,16},{16,18},{18... | collective-permute-start | bytes 3145736 | tf_op jit(solution)/shard_map/ppermute | solution.py:15
  10.1 3.3 %collective-permute-start.1 = (bf16[2,1024,256]{2,1,0:T(8,128)(2,1)}, bf16[2,1024,256]{2,1,0:T(8,128)(2,1)}, u32[]{:S(2)}, u32[]{:S(2)}) collective-permute-start(bf16[2,1024,256]{2,1,0:T(8,128)(2,1)} %param.9), channel_id=1, source_target_pairs={{2,0},{4,2},{6,4},{8,6},{10,8},{12,10},{14,12},{16,14},{18,16},{20... | collective-permute-start | bytes 3145736 | tf_op jit(solution)/shard_map/ppermute | solution.py:17
  13.4 0.8 slice_bitcast_fusion.1
  14.2 21.6 %collective-permute-done = bf16[2,1024,256]{2,1,0:T(8,128)(2,1)} collective-permute-done((bf16[2,1024,256]{2,1,0:T(8,128)(2,1)}, bf16[2,1024,256]{2,1,0:T(8,128)(2,1)}, u32[]{:S(2)}, u32[]{:S(2)}) %collective-permute-start) | collective-permute-done | bytes 1048608 | tf_op jit(solution)/shard_map/ppermute | solution.py:15
  35.8 1.3 constant_dynamic-update-slice_fusion.2
  37.1 1.3 constant_dynamic-update-slice_fusion.1
  38.4 18.7 %collective-permute-done.1 = bf16[2,1024,256]{2,1,0:T(8,128)(2,1)} collective-permute-done((bf16[2,1024,256]{2,1,0:T(8,128)(2,1)}, bf16[2,1024,256]{2,1,0:T(8,128)(2,1)}, u32[]{:S(2)}, u32[]{:S(2)}) %collective-permute-start.1) | collective-permute-done | bytes 1048608 | tf_op jit(solution)/shard_map/ppermute | solution.py:17
  57.1 1.3 constant_dynamic-update-slice_fusion
  58.4 4.6 %gather_fusion = bf16[16,1024,256]{2,1,0:T(8,128)(2,1)} fusion(bf16[6,1024,256]{2,1,0:T(8,128)(2,1)S(1)} %constant_dynamic-update-slice_fusion, s32[1024]{0:T(1024)S(1)} %get-tuple-element.14), kind=kCustom, calls=%fused_computation | custom fusion | bytes 16777280 | tf_op jit(solution)/shard_map/gather | solution.py:70
  63.0 4.7 %gather_fusion.1 = bf16[16,1024,256]{2,1,0:T(8,128)(2,1)} fusion(bf16[6,1024,256]{2,1,0:T(8,128)(2,1)S(1)} %constant_dynamic-update-slice_fusion, s32[1024]{0:T(1024)S(1)} %get-tuple-element.13), kind=kCustom, calls=%fused_computation.1 | custom fusion | bytes 16777280 | tf_op jit(solution)/shard_map/gather | solution.py:71
  67.7 10.2 %fusion.23 = f32[16,256,256]{2,1,0:T(8,128)} fusion(bf16[16,1024,256]{2,1,0:T(8,128)(2,1)} %gather_fusion, bf16[16,1024,256]{2,1,0:T(8,128)(2,1)} %gather_fusion.1), kind=kOutput, calls=%fused_computation.41 | convolution fusion | flops 2147483648 | bytes 20971520 | tf_op jit(solution)/shard_map/pqa,pqb->pab/dot_general | solution.py:72
  78.0 0.1 copy.18
  78.1 0.5 copy-done.5
  78.8 0.7 copy-done.2
  79.5 12.1 %broadcast_multiply_fusion = f32[16,4,128,256]{3,2,1,0:T(8,128)} fusion(f32[16,4]{1,0:T(8,128)S(1)} %copy.18, bf16[16,4,256,256]{3,2,1,0:T(8,128)(2,1)} %param.13, s32[]{:T(128)S(6)} %select_n.48, bf16[16,256,256]{2,1,0:T(8,128)(2,1)S(1)} %copy-done.2), kind=kOutput, calls=%fused_computation.3 | convolution fusion | flops 2151677952 | bytes 23068932 | tf_op jit(solution)/shard_map/pcal,pcbl->pcab/dot_general | solution.py:35
  91.5 3.5 %broadcast_in_dim.22 = f32[48,128,256]{2,1,0:T(8,128)} broadcast(f32[]{:T(128)} %constant.7.clone.1), dimensions={} | broadcast | bytes 6291460 | tf_op jit(solution)/shard_map/broadcast_in_dim | solution.py:46
  95.0 20.1 %scatter_fusion = f32[48,128,256]{2,1,0:T(8,128)} fusion(f32[48,128,256]{2,1,0:T(8,128)} %broadcast_in_dim.22, s32[64]{0:T(128)S(1)} %fusion.21, f32[64,128,256]{2,1,0:T(8,128)} %bitcast.20), kind=kCustom, calls=%fused_computation.2 | custom fusion | flops 2097152 | bytes 25166080 | tf_op jit(solution)/shard_map/scatter-add | solution.py:47
  115.1 2.6 %fusion.22 = (f32[16,128,256]{2,1,0:T(8,128)S(1)}, f32[16,128,256]{2,1,0:T(8,128)S(1)}) fusion(f32[48,128,256]{2,1,0:T(8,128)} %scatter_fusion), kind=kLoop, calls=%fused_computation.40 | loop fusion | bytes 8388608 | tf_op jit(solution)/shard_map/slice | solution.py:96
  117.7 2.5 %collective-permute-start.2 = (f32[16,128,256]{2,1,0:T(8,128)S(1)}, f32[16,128,256]{2,1,0:T(8,128)}, u32[]{:S(2)}, u32[]{:S(2)}) collective-permute-start(f32[16,128,256]{2,1,0:T(8,128)S(1)} %get-tuple-element.7), channel_id=1, source_target_pairs={{0,2},{2,4},{4,6},{6,8},{8,10},{10,12},{12,14},{14,16},{16,18},{18... | collective-permute-start | bytes 6291464 | tf_op jit(solution)/shard_map/ppermute | solution.py:27
  120.2 5.5 %collective-permute-start.3 = (f32[16,128,256]{2,1,0:T(8,128)S(1)}, f32[16,128,256]{2,1,0:T(8,128)}, u32[]{:S(2)}, u32[]{:S(2)}) collective-permute-start(f32[16,128,256]{2,1,0:T(8,128)S(1)} %get-tuple-element.8), channel_id=1, source_target_pairs={{2,0},{4,2},{6,4},{8,6},{10,8},{12,10},{14,12},{16,14},{18,16},{20... | collective-permute-start | bytes 6291464 | tf_op jit(solution)/shard_map/ppermute | solution.py:27
  125.7 0.2 select_reduce_fusion
  126.1 44.3 %collective-permute-done.2 = f32[16,128,256]{2,1,0:T(8,128)} collective-permute-done((f32[16,128,256]{2,1,0:T(8,128)S(1)}, f32[16,128,256]{2,1,0:T(8,128)}, u32[]{:S(2)}, u32[]{:S(2)}) %collective-permute-start.2) | collective-permute-done | bytes 2097184 | tf_op jit(solution)/shard_map/ppermute | solution.py:27
  170.4 42.8 %collective-permute-done.3 = f32[16,128,256]{2,1,0:T(8,128)} collective-permute-done((f32[16,128,256]{2,1,0:T(8,128)S(1)}, f32[16,128,256]{2,1,0:T(8,128)}, u32[]{:S(2)}, u32[]{:S(2)}) %collective-permute-start.3) | collective-permute-done | bytes 2097184 | tf_op jit(solution)/shard_map/ppermute | solution.py:27
  213.2 4.9 %fusion.13 = f32[16,128,256]{2,1,0:T(8,128)} fusion(f32[16,128,256]{2,1,0:T(8,128)} %collective-permute-done.3, f32[16,128,256]{2,1,0:T(8,128)} %collective-permute-done.2, f32[48,128,256]{2,1,0:T(8,128)} %scatter_fusion, f32[16,256,256]{2,1,0:T(8,128)} %all-reduce.2.cloned.1.call-done, s32[]{:T(128)S(6)} %select_n.48, f32[16,256]{1,0:T(8,128)S(1)} %fusion.16, ...), kind=kLoop, calls=%fused_computation.12 | loop fusion | flops 5242880 | bytes 11583556 | tf_op jit(solution)/shard_map/mul | solution.py:103
  (26 shorter events, 0.5 us)
Async XLA Ops:
  6.5 71.4 %copy-start = (f32[256,4]{0,1:T(4,128)S(1)}, f32[256,4]{0,1:T(4,128)}, u32[]{:S(2)}) copy-start(f32[256,4]{0,1:T(4,128)} %param.15) | copy-start | bytes 12292
  6.5 206.7 %all-reduce.2.cloned.1.call-start = ((), (), s32[]{:S(2)}) async-start(), calls=%async_computation | async-start | bytes 8388608 | tf_op jit(solution)/shard_map/psum | solution.py:75
  6.5 29.3 %collective-permute-start = (bf16[2,1024,256]{2,1,0:T(8,128)(2,1)}, bf16[2,1024,256]{2,1,0:T(8,128)(2,1)}, u32[]{:S(2)}, u32[]{:S(2)}) collective-permute-start(bf16[2,1024,256]{2,1,0:T(8,128)(2,1)} %param.9), channel_id=1, source_target_pairs={{0,2},{2,4},{4,6},{6,8},{8,10},{10,12},{12,14},{14,16},{16,18},{18... | collective-permute-start | bytes 3145736 | tf_op jit(solution)/shard_map/ppermute | solution.py:15
  10.1 47.0 %collective-permute-start.1 = (bf16[2,1024,256]{2,1,0:T(8,128)(2,1)}, bf16[2,1024,256]{2,1,0:T(8,128)(2,1)}, u32[]{:S(2)}, u32[]{:S(2)}) collective-permute-start(bf16[2,1024,256]{2,1,0:T(8,128)(2,1)} %param.9), channel_id=1, source_target_pairs={{2,0},{4,2},{6,4},{8,6},{10,8},{12,10},{14,12},{16,14},{18,16},{20... | collective-permute-start | bytes 3145736 | tf_op jit(solution)/shard_map/ppermute | solution.py:17
  77.9 0.7 copy-start.5
  77.9 1.6 copy-start.2
  115.1 10.6 %copy-start.6 = (f32[32]{0:T(128)S(1)}, f32[32]{0:T(128)}, u32[]{:S(2)}) copy-start(f32[32]{0:T(128)} %param.17) | copy-start | bytes 388
  115.1 10.8 %copy-start.3 = (f32[16,256]{1,0:T(8,128)S(1)}, f32[16,256]{1,0:T(8,128)}, u32[]{:S(2)}) copy-start(f32[16,256]{1,0:T(8,128)} %param.16) | copy-start | bytes 49156
  115.1 10.9 %copy-start.4 = (s32[16]{0:T(128)S(1)}, s32[16]{0:T(128)}, u32[]{:S(2)}) copy-start(s32[16]{0:T(128)} %param.11) | copy-start | bytes 196
  117.7 52.7 %collective-permute-start.2 = (f32[16,128,256]{2,1,0:T(8,128)S(1)}, f32[16,128,256]{2,1,0:T(8,128)}, u32[]{:S(2)}, u32[]{:S(2)}) collective-permute-start(f32[16,128,256]{2,1,0:T(8,128)S(1)} %get-tuple-element.7), channel_id=1, source_target_pairs={{0,2},{2,4},{4,6},{6,8},{8,10},{10,12},{12,14},{14,16},{16,18},{18... | collective-permute-start | bytes 6291464 | tf_op jit(solution)/shard_map/ppermute | solution.py:27
  120.2 93.0 %collective-permute-start.3 = (f32[16,128,256]{2,1,0:T(8,128)S(1)}, f32[16,128,256]{2,1,0:T(8,128)}, u32[]{:S(2)}, u32[]{:S(2)}) collective-permute-start(f32[16,128,256]{2,1,0:T(8,128)S(1)} %get-tuple-element.8), channel_id=1, source_target_pairs={{2,0},{4,2},{6,4},{8,6},{10,8},{12,10},{14,12},{16,14},{18,16},{20... | collective-permute-start | bytes 6291464 | tf_op jit(solution)/shard_map/ppermute | solution.py:27
  126.0 92.1 %copy-start.1 = (f32[256,4]{0,1:T(4,128)S(1)}, f32[256,4]{0,1:T(4,128)}, u32[]{:S(2)}) copy-start(f32[256,4]{0,1:T(4,128)} %param.15) | copy-start | bytes 12292
Sparse Core Ops, SparseCore 0:
  78.0 29.6 all-reduce.1
where the time goes:
time: 226 us; the launch traced here: 225 us
  waiting for transfers between devices  127 us (56%)
  other arithmetic  26.2 us (12%)
  matrix products  22.3 us (10%)
  local copies, waits for them, and re-layouts  20.7 us (9%)
  starting transfers between devices  14.8 us (7%)
  between operations  13.5 us (6%)
    ppermute x2, waiting for transfers between devices, passed_along(): lax.ppermute(value, axis, [(source, source + steps) for source in range(l...  87.1 us
    ppermute x1, waiting for transfers between devices, with_halo(): lax.ppermute(tail, axis, [(i, (i + 1) % count) for i in range(ends)])  21.6 us
    scatter-add x1, other arithmetic, route_terms(): return empty.at[flat_slots].add(flat_terms, mode='drop')  20.1 us
    ppermute x1, waiting for transfers between devices, with_halo(): lax.ppermute(head, axis, [((i + 1) % count, i) for i in range(ends)])  18.7 us
    dot_general x1, matrix products, coupling_terms(): jnp.einsum('pcal,pcbl->pcab', first_product, source_margins, preferred_el...  12.1 us
    dot_general x1, matrix products, local(): jnp.einsum('pqa,pqb->pab', left_block, right_block, preferred_element_typ...  10.2 us
    ppermute x2, starting transfers between devices, passed_along(): lax.ppermute(value, axis, [(source, source + steps) for source in range(l...  7.98 us
    mul x1, other arithmetic, local(): return (base_terms + coupling) * row_mask[:, :, None] * col_mask[:, None, :]  4.94 us
  transfers between devices with their start and end apart: 5, of which 4 were waited for; matrix products, arithmetic and copies ran while one was open for 19% of the time, Pallas kernels for 0%

commit v1 on v0

v1 whole, which is shorter than its diff:
```python
import jax
import jax.numpy as jnp
from jax import lax
from jax.experimental import pallas as pl
from jax.experimental.pallas import tpu as pltpu
from jax.sharding import PartitionSpec as P

MIB = 2**20


def term_kernel(core, slots, weights, margins, amps, low, mid, high, sums):
    source = pl.program_id(0)
    pairs, rows = low.shape[0], low.shape[1]

    @pl.when(source == 0)
    def _():
        sums[...] = jnp.zeros_like(sums)

    start = pl.multiple_of(core[0] * rows, rows)
    for c in range(margins.shape[1]):
        first = jnp.dot(
            margins[0, c, pl.ds(start, rows), :], amps[0], preferred_element_type=jnp.float32
        ).astype(jnp.bfloat16)
        term = lax.dot_general(
            first, margins[0, c], (((1,), (1,)), ((), ())), preferred_element_type=jnp.float32
        )
        slot = slots[source, c]
        sums[slot] += term * weights[source, c]

    @pl.when(source == pl.num_programs(0) - 1)
    def _():
        low[...] = sums[0:pairs].astype(low.dtype)
        mid[...] = sums[pairs : 2 * pairs]
        high[...] = sums[2 * pairs : 3 * pairs].astype(high.dtype)


def coupling_sums(core, slots, weights, margins, amps, rows):
    pairs, couples, width, _ = margins.shape
    whole = pl.BlockSpec((pairs, rows, width), lambda q, *_: (0, 0, 0))
    flops = 4 * pairs * couples * rows * width * width
    return pl.pallas_call(
        term_kernel,
        grid_spec=pltpu.PrefetchScalarGridSpec(
            num_scalar_prefetch=3,
            grid=(pairs,),
            in_specs=[
                pl.BlockSpec((1, couples, width, width), lambda q, *_: (q, 0, 0, 0)),
                pl.BlockSpec((1, width, width), lambda q, *_: (q, 0, 0)),
            ],
            out_specs=[whole, whole, whole],
            scratch_shapes=[pltpu.VMEM((3 * pairs, rows, width), jnp.float32)],
        ),
        out_shape=[
            jax.ShapeDtypeStruct((pairs, rows, width), jnp.bfloat16),
            jax.ShapeDtypeStruct((pairs, rows, width), jnp.float32),
            jax.ShapeDtypeStruct((pairs, rows, width), jnp.bfloat16),
        ],
        compiler_params=pltpu.CompilerParams(vmem_limit_bytes=32 * MIB),
        cost_estimate=pl.CostEstimate(
            flops=flops, bytes_accessed=2 * margins.size + 2 * amps.size, transcendentals=0
        ),
        name="coupling_sums",
    )(core, slots, weights, margins, amps)


def product_kernel(core, left, right, mine, other, full):
    rows = mine.shape[1]
    for i in range(left.shape[0]):
        for j in range(right.shape[0]):
            full[i * right.shape[0] + j] = lax.dot_general(
                left[i], right[j], (((0,), (0,)), ((), ())), preferred_element_type=jnp.float32
            )
    here = pl.multiple_of(core[0] * rows, rows)
    there = pl.multiple_of((1 - core[0]) * rows, rows)
    mine[...] = full[:, pl.ds(here, rows), :]
    other[...] = full[:, pl.ds(there, rows), :]


def products(core, left, right, rows):
    count, width = left.shape[0] * right.shape[0], left.shape[2]
    half = jax.ShapeDtypeStruct((count, rows, width), jnp.float32)
    vmem = pl.BlockSpec(memory_space=pltpu.VMEM)
    return pl.pallas_call(
        product_kernel,
        in_specs=[pl.BlockSpec(memory_space=pltpu.SMEM), vmem, vmem],
        out_specs=[vmem, vmem],
        out_shape=[half, half],
        scratch_shapes=[pltpu.VMEM((count, width, width), jnp.float32)],
        compiler_params=pltpu.CompilerParams(vmem_limit_bytes=24 * MIB),
        cost_estimate=pl.CostEstimate(
            flops=2 * count * left.shape[1] * width * width,
            bytes_accessed=4 * left.size + 8 * count * rows * width,
            transcendentals=0,
        ),
        name="orbital_products",
    )(core, left, right)


def base_kernel(core, table, shift, counts, near, energy, amps, mid, low, high, out):
    pair = pl.program_id(0)
    rows, width = out.shape[1], out.shape[2]
    start = pl.multiple_of(core[0] * rows, rows)
    across = energy[0, 0:1, :]
    down = jnp.broadcast_to(energy[0, 0:1, pl.ds(start, rows)], (rows, rows)).T[:, 0:1]
    denominator = down + across - shift[pair]
    total = near[table[pair]] + denominator * amps[0].astype(jnp.float32)
    total += mid[0] + low[0].astype(jnp.float32) + high[0].astype(jnp.float32)
    row = lax.broadcasted_iota(jnp.int32, (rows, width), 0) + start
    col = lax.broadcasted_iota(jnp.int32, (rows, width), 1)
    inside = (row < counts[pair]) & (col < counts[pair])
    out[0] = jnp.where(inside, total, 0.0)


def assemble(core, table, shift, counts, near, energy, amps, mid, low, high):
    pairs, rows, width = mid.shape
    one = pl.BlockSpec((1, rows, width), lambda p, *_: (p, 0, 0))
    return pl.pallas_call(
        base_kernel,
        grid_spec=pltpu.PrefetchScalarGridSpec(
            num_scalar_prefetch=4,
            grid=(pairs,),
            in_specs=[
                pl.BlockSpec(near.shape, lambda p, *_: (0, 0, 0)),
                pl.BlockSpec((1, 1, width), lambda p, *_: (p, 0, 0)),
                pl.BlockSpec((1, rows, width), lambda p, core, *_: (p, core[0], 0)),
                one,
                one,
                one,
            ],
            out_specs=one,
        ),
        out_shape=jax.ShapeDtypeStruct((pairs, rows, width), jnp.float32),
        compiler_params=pltpu.CompilerParams(vmem_limit_bytes=24 * MIB),
        cost_estimate=pl.CostEstimate(
            flops=8 * mid.size, bytes_accessed=16 * mid.size, transcendentals=0
        ),
        name="assemble",
    )(core, table, shift, counts, near, energy[:, None, :], amps, mid, low, high)


def local(
    blocks,
    pair_orbs,
    pno_count,
    amplitudes,
    margins,
    couple_target,
    couple_weight,
    pno_energy,
    occ_energy,
):
    holder = lax.axis_index("pairs")
    count = lax.axis_size("pairs")
    core = lax.axis_index("aux").astype(jnp.int32)
    pairs, width = amplitudes.shape[0], amplitudes.shape[2]
    orbs = blocks.shape[0]
    rows = width // lax.axis_size("aux")
    up = [(i, i + 1) for i in range(count - 1)]
    down = [(i + 1, i) for i in range(count - 1)]
    swap = [(0, 1), (1, 0)]
    where = core.reshape(1)

    below = lax.ppermute(blocks, "pairs", up)

    slots = lax.dynamic_slice_in_dim(couple_target, holder * pairs, pairs, 0)
    slots = jnp.clip(slots - (holder - 1) * pairs, 0, 3 * pairs - 1)
    weights = lax.dynamic_slice_in_dim(couple_weight, holder * pairs, pairs, 0)
    low, mid, high = coupling_sums(where, slots, weights, margins, amplitudes, rows)
    below, mid = lax.optimization_barrier((below, mid))
    from_upper = lax.ppermute(low, "pairs", down)
    from_lower = lax.ppermute(high, "pairs", up)

    own_mine, own_other = products(where, blocks, blocks, rows)
    own = own_mine + lax.ppermute(own_other, "aux", swap)

    back_mine, back_other = products(where, below, blocks, rows)
    back = (back_mine + lax.ppermute(back_other, "aux", swap)).astype(jnp.bfloat16)
    above = lax.ppermute(back, "pairs", down).astype(jnp.float32)
    left_mine, left_other = products(where, blocks, below, rows)
    left = left_mine + lax.ppermute(left_other, "aux", swap)

    near = jnp.concatenate([left, own, above], axis=0)
    first = pair_orbs[:, 0] - holder * orbs
    second = pair_orbs[:, 1] - (holder - 1) * orbs
    table = (second // orbs) * (orbs * orbs) + first * orbs + second % orbs
    orbitals = jnp.arange(occ_energy.shape[0], dtype=jnp.int32)
    pick = lambda o: jnp.sum(jnp.where(o[:, None] == orbitals[None, :], occ_energy[None, :], 0.0), axis=1)
    shift = pick(pair_orbs[:, 0]) + pick(pair_orbs[:, 1])
    return assemble(
        where, table, shift, pno_count, near, pno_energy, amplitudes, mid, from_lower, from_upper
    )


def solution(mesh):
    placed = (
        P("pairs", "aux", None),
        P("pairs", None),
        P("pairs"),
        P("pairs", None, None),
        P("pairs", None, None, None),
        P(),
        P(),
        P("pairs", None),
        P(),
    )
    return jax.shard_map(
        local, mesh=mesh, in_specs=placed, out_specs=P("pairs", "aux", None), check_vma=False
    )
```

time: 226 us -> 101 us (0.45)
  waiting for transfers between devices: 127 us -> 49.8 us
  Pallas kernels: 0 us -> 25.9 us
  other arithmetic: 26.2 us -> 2.81 us
  matrix products: 22.3 us -> 0 us
  between operations: 13.5 us -> 0.24 us
  local copies, waits for them, and re-layouts: 20.7 us -> 7.48 us
    ppermute x4 -> x7, waiting for transfers between devices: 127 us -> 49.8 us  [the longest x1 42.2 us: local(): above = lax.ppermute(back, 'pairs', down).astype(jnp.float32)]
    pallas_call x0 -> x5, Pallas kernels: none -> 25.9 us  [the longest x1 11 us: coupling_sums(): pl.pallas_call(term_kernel, grid_spec=pltpu.PrefetchScalarGridSpec(num_sc...]
    dot_general x2 -> x0, matrix products: 22.3 us -> none  [the longest x1 12.1 us: coupling_terms(): jnp.einsum('pcal,pcbl->pcab', first_product, source_margins, preferred_el...]
    scatter-add x1 -> x0, other arithmetic: 20.1 us -> none  [route_terms(): return empty.at[flat_slots].add(flat_terms, mode='drop')]
    gather x2 -> x0, local copies, waits for them, and re-layouts: 9.29 us -> none  [the longest x1 4.66 us: local(): right_block = padded[pair_orbs[:, 1] - base_orb]]
    mul x1 -> x0, other arithmetic: 4.94 us -> none  [local(): return (base_terms + coupling) * row_mask[:, :, None] * col_mask[:, None, :]]
    broadcast_in_dim x1, local copies, waits for them, and re-layouts: 3.45 us -> 0.01 us  [assemble(): energy[:, None, :]]
    unnamed x16 -> x26, local copies, waits for them, and re-layouts: 3.74 us -> 6.63 us
  transfers between devices with their start and end apart: 5 -> 7, of which waited for: 4 -> 2; matrix products, arithmetic and copies ran while one was open for 19% -> 4% of each run, Pallas kernels for 0% -> 14%
where the time goes in v1:
time: 101 us; the launch traced here: 98.9 us
  waiting for transfers between devices  49.8 us (49%)
  Pallas kernels  25.9 us (26%)
  starting transfers between devices  12.8 us (13%)
  local copies, waits for them, and re-layouts  7.48 us (7%)
  other arithmetic  2.81 us (3%)
    ppermute x1, waiting for transfers between devices, local(): above = lax.ppermute(back, 'pairs', down).astype(jnp.float32)  42.2 us
    pallas_call x1, Pallas kernels, coupling_sums(): pl.pallas_call(term_kernel, grid_spec=pltpu.PrefetchScalarGridSpec(num_sc...  11 us
    pallas_call x1, Pallas kernels, assemble(): pl.pallas_call(base_kernel, grid_spec=pltpu.PrefetchScalarGridSpec(num_sc...  10.9 us
    ppermute x1, waiting for transfers between devices, local(): below = lax.ppermute(blocks, 'pairs', up)  7.54 us
    unnamed x26, local copies, waits for them, and re-layouts  6.63 us
    ppermute x1, starting transfers between devices, local(): from_upper = lax.ppermute(low, 'pairs', down)  4.24 us
    pallas_call x3, Pallas kernels, products(): pl.pallas_call(product_kernel, in_specs=[pl.BlockSpec(memory_space=pltpu....  4.08 us
    ppermute x1, starting transfers between devices, local(): below = lax.ppermute(blocks, 'pairs', up)  3.52 us
  transfers between devices with their start and end apart: 7, of which 2 were waited for; matrix products, arithmetic and copies ran while one was open for 4% of the time, Pallas kernels for 14%

profile of v1, /device:TPU:12, one launch (start us, length us, event | category | flops | bytes accessed | tf_op | source)
XLA Modules:
  0.0 98.9 jit_solution(3755337366481952639)
XLA Ops:
  0.0 3.5 %collective-permute-start = (bf16[2,1024,256]{2,1,0:T(8,128)(2,1)}, bf16[2,1024,256]{2,1,0:T(8,128)(2,1)S(1)}, u32[]{:S(2)}, u32[]{:S(2)}) collective-permute-start(bf16[2,1024,256]{2,1,0:T(8,128)(2,1)} %right.3), channel_id=1, source_target_pairs={{0,2},{2,4},{4,6},{6,8},{8,10},{10,12},{12,14},{14,16},{16,18},{18... | collective-permute-start | bytes 3145736 | tf_op jit(solution)/shard_map/ppermute | solution.py:163
  3.5 0.1 constant_dynamic-slice_fusion.1
  3.6 0.1 copy.14
  3.7 0.8 constant_dynamic-slice_fusion
  4.5 0.1 copy.15.weights
  4.6 3.4 %copy-done.2 = bf16[16,4,256,256]{3,2,1,0:T(8,128)(2,1)S(1)} copy-done((bf16[16,4,256,256]{3,2,1,0:T(8,128)(2,1)S(1)}, bf16[16,4,256,256]{3,2,1,0:T(8,128)(2,1)}, u32[]{:S(2)}) %copy-start.2) | copy-done | bytes 8388632
  7.9 1.6 %copy-done.3 = bf16[16,256,256]{2,1,0:T(8,128)(2,1)S(1)} copy-done((bf16[16,256,256]{2,1,0:T(8,128)(2,1)S(1)}, bf16[16,256,256]{2,1,0:T(8,128)(2,1)}, u32[]{:S(2)}) %copy-start.3) | copy-done | bytes 2097176
  9.5 11.0 %coupling_sums.1 = (bf16[16,128,256]{2,1,0:T(8,128)(2,1)}, f32[16,128,256]{2,1,0:T(8,128)S(1)}, bf16[16,128,256]{2,1,0:T(8,128)(2,1)}) custom-call(s32[1]{0:T(128)} %bitcast.core, s32[16,4]{1,0:T(8,128)S(1)} %subtract_clamp_fusion.slots, f32[16,4]{1,0:T(8,128)S(1)} %copy.15.weights, bf16[16,4,256,256]{3,2,1,0:T(8,128)(2,1)S(1)} %copy-done.2, ...), custom_call_target="tpu_custom_call" | custom-call | flops 2147483648 | bytes 10485760 | tf_op jit(solution)/shard_map/coupling_sums/pallas_call | solution.py:41
  20.5 7.5 %collective-permute-done.right.left = bf16[2,1024,256]{2,1,0:T(8,128)(2,1)S(1)} collective-permute-done((bf16[2,1024,256]{2,1,0:T(8,128)(2,1)}, bf16[2,1024,256]{2,1,0:T(8,128)(2,1)S(1)}, u32[]{:S(2)}, u32[]{:S(2)}) %collective-permute-start) | collective-permute-done | bytes 1048608 | tf_op jit(solution)/shard_map/ppermute | solution.py:163
  28.0 0.8 orbital_products.5
  29.0 2.5 %collective-permute-start.5 = (bf16[16,128,256]{2,1,0:T(8,128)(2,1)}, bf16[16,128,256]{2,1,0:T(8,128)(2,1)}, u32[]{:S(2)}, u32[]{:S(2)}) collective-permute-start(bf16[16,128,256]{2,1,0:T(8,128)(2,1)} %get-tuple-element.25), channel_id=1, source_target_pairs={{0,2},{2,4},{4,6},{6,8},{8,10},{10,12},{12,14},{14,16},{16,18},{18... | collective-permute-start | bytes 3145736 | tf_op jit(solution)/shard_map/ppermute | solution.py:171
  31.5 4.2 %collective-permute-start.6 = (bf16[16,128,256]{2,1,0:T(8,128)(2,1)}, bf16[16,128,256]{2,1,0:T(8,128)(2,1)}, u32[]{:S(2)}, u32[]{:S(2)}) collective-permute-start(bf16[16,128,256]{2,1,0:T(8,128)(2,1)} %get-tuple-element.26), channel_id=1, source_target_pairs={{2,0},{4,2},{6,4},{8,6},{10,8},{12,10},{14,12},{16,14},{18,16},{20... | collective-permute-start | bytes 3145736 | tf_op jit(solution)/shard_map/ppermute | solution.py:170
  35.7 1.6 %orbital_products.4 = (f32[4,128,256]{2,1,0:T(8,128)S(1)}, f32[4,128,256]{2,1,0:T(8,128)}) custom-call(s32[1]{0:T(128)} %bitcast.core, bf16[2,1024,256]{2,1,0:T(8,128)(2,1)S(1)} %copy-done.1, bf16[2,1024,256]{2,1,0:T(8,128)(2,1)S(1)} %copy-done.1), custom_call_target="tpu_custom_call" | custom-call | flops 536870912 | bytes 3145728 | tf_op jit(solution)/shard_map/orbital_products/pallas_call | solution.py:83
  37.4 1.6 %orbital_products.3 = (f32[4,128,256]{2,1,0:T(8,128)S(1)}, f32[4,128,256]{2,1,0:T(8,128)}) custom-call(s32[1]{0:T(128)} %bitcast.core, bf16[2,1024,256]{2,1,0:T(8,128)(2,1)S(1)} %copy-done.1, bf16[2,1024,256]{2,1,0:T(8,128)(2,1)S(1)} %collective-permute-done.right.left), custom_call_target="tpu_custom_call" | custom-call | flops 536870912 | bytes 3145728 | tf_op jit(solution)/shard_map/orbital_products/pallas_call | solution.py:83
  39.0 0.5 collective-permute-start.1
  39.5 0.1 add_convert_fusion
  39.6 1.9 %collective-permute-start.4 = (bf16[4,128,256]{2,1,0:T(8,128)(2,1)S(1)}, bf16[4,128,256]{2,1,0:T(8,128)(2,1)S(1)}, u32[]{:S(2)}, u32[]{:S(2)}) collective-permute-start(bf16[4,128,256]{2,1,0:T(8,128)(2,1)S(1)} %add_convert_fusion), channel_id=1, source_target_pairs={{2,0},{4,2},{6,4},{8,6},{10,8},{12,10},{14,12},{16,14},{18,16},{20... | collective-permute-start | bytes 786440 | tf_op jit(solution)/shard_map/ppermute | solution.py:178
  41.6 0.2 select_reduce_fusion
  41.8 1.3 %add.36 = f32[4,128,256]{2,1,0:T(8,128)S(1)} add(f32[4,128,256]{2,1,0:T(8,128)} %copy-done.5, f32[4,128,256]{2,1,0:T(8,128)} %collective-permute-done.2) | non-fusion elementwise | flops 131072 | bytes 1572864 | tf_op jit(solution)/shard_map/add | solution.py:174
  43.1 1.1 %add.35 = f32[4,128,256]{2,1,0:T(8,128)S(1)} add(f32[4,128,256]{2,1,0:T(8,128)S(1)} %copy-done.7, f32[4,128,256]{2,1,0:T(8,128)} %collective-permute-done.1) | non-fusion elementwise | flops 131072 | bytes 1572864 | tf_op jit(solution)/shard_map/add | solution.py:180
  44.2 42.2 %collective-permute-done.4 = bf16[4,128,256]{2,1,0:T(8,128)(2,1)S(1)} collective-permute-done((bf16[4,128,256]{2,1,0:T(8,128)(2,1)S(1)}, bf16[4,128,256]{2,1,0:T(8,128)(2,1)S(1)}, u32[]{:S(2)}, u32[]{:S(2)}) %collective-permute-start.4) | collective-permute-done | bytes 262176 | tf_op jit(solution)/shard_map/ppermute | solution.py:178
  86.5 0.1 pad_maximum_fusion.near
  86.6 1.4 %copy-done.4 = bf16[16,256,256]{2,1,0:T(8,128)(2,1)S(1)} copy-done((bf16[16,256,256]{2,1,0:T(8,128)(2,1)S(1)}, bf16[16,256,256]{2,1,0:T(8,128)(2,1)}, u32[]{:S(2)}) %copy-start.4) | copy-done | bytes 2097176
  88.1 10.9 %assemble.1 = f32[16,128,256]{2,1,0:T(8,128)} custom-call(s32[1]{0:T(128)} %bitcast.core, s32[16]{0:T(128)S(1)} %fusion.table, f32[16]{0:T(128)S(1)} %add.33.shift, s32[16]{0:T(128)S(1)} %copy-done.8, f32[12,128,256]{2,1,0:T(8,128)S(1)} %pad_maximum_fusion.near, f32[16,1,256]{2,1,0:T(1,128)S(1)} %broadcast_in_dim.25.energy, ...), custom_call_target="tpu_custom_call" | custom-call | flops 4194304 | bytes 8388608 | tf_op jit(solution)/shard_map/assemble/pallas_call | solution.py:117
  (34 shorter events, 0.2 us)
Async XLA Ops:
  0.0 3.5 %copy-start = (s32[256,4]{0,1:T(4,128)S(1)}, s32[256,4]{0,1:T(4,128)}, u32[]{:S(2)}) copy-start(s32[256,4]{0,1:T(4,128)} %param.14) | copy-start | bytes 12292
  0.0 28.0 %collective-permute-start = (bf16[2,1024,256]{2,1,0:T(8,128)(2,1)}, bf16[2,1024,256]{2,1,0:T(8,128)(2,1)S(1)}, u32[]{:S(2)}, u32[]{:S(2)}) collective-permute-start(bf16[2,1024,256]{2,1,0:T(8,128)(2,1)} %right.3), channel_id=1, source_target_pairs={{0,2},{2,4},{4,6},{6,8},{8,10},{10,12},{12,14},{14,16},{16,18},{18... | collective-permute-start | bytes 3145736 | tf_op jit(solution)/shard_map/ppermute | solution.py:163
  4.6 3.4 %copy-start.2 = (bf16[16,4,256,256]{3,2,1,0:T(8,128)(2,1)S(1)}, bf16[16,4,256,256]{3,2,1,0:T(8,128)(2,1)}, u32[]{:S(2)}) copy-start(bf16[16,4,256,256]{3,2,1,0:T(8,128)(2,1)} %margins.1) | copy-start | bytes 25165828
  7.9 1.6 %copy-start.3 = (bf16[16,256,256]{2,1,0:T(8,128)(2,1)S(1)}, bf16[16,256,256]{2,1,0:T(8,128)(2,1)}, u32[]{:S(2)}) copy-start(bf16[16,256,256]{2,1,0:T(8,128)(2,1)} %amps.3) | copy-start | bytes 6291460
  9.5 18.5 %copy-start.1 = (bf16[2,1024,256]{2,1,0:T(8,128)(2,1)S(1)}, bf16[2,1024,256]{2,1,0:T(8,128)(2,1)}, u32[]{:S(2)}) copy-start(bf16[2,1024,256]{2,1,0:T(8,128)(2,1)} %right.3) | copy-start | bytes 3145732
  28.9 8.5 %copy-start.10 = (s32[16,2]{0,1:T(2,128)S(1)}, s32[16,2]{0,1:T(2,128)}, u32[]{:S(2)}) copy-start(s32[16,2]{0,1:T(2,128)} %param.10) | copy-start | bytes 388
  28.9 10.6 %collective-permute-start.3 = (f32[4,128,256]{2,1,0:T(8,128)S(1)}, f32[4,128,256]{2,1,0:T(8,128)S(1)}, u32[]{:S(2)}, u32[]{:S(2)}) collective-permute-start(f32[4,128,256]{2,1,0:T(8,128)S(1)} %get-tuple-element.23), channel_id=1, source_target_pairs={{0,1},{1,0},{2,3},{3,2},{4,5},{5,4},{6,7},{7,6},{8,9},{9,8},{10,11... | collective-permute-start | bytes 1572872 | tf_op jit(solution)/shard_map/ppermute | solution.py:177
  29.0 57.7 %collective-permute-start.5 = (bf16[16,128,256]{2,1,0:T(8,128)(2,1)}, bf16[16,128,256]{2,1,0:T(8,128)(2,1)}, u32[]{:S(2)}, u32[]{:S(2)}) collective-permute-start(bf16[16,128,256]{2,1,0:T(8,128)(2,1)} %get-tuple-element.25), channel_id=1, source_target_pairs={{0,2},{2,4},{4,6},{6,8},{8,10},{10,12},{12,14},{14,16},{16,18},{18... | collective-permute-start | bytes 3145736 | tf_op jit(solution)/shard_map/ppermute | solution.py:171
  31.5 55.2 %collective-permute-start.6 = (bf16[16,128,256]{2,1,0:T(8,128)(2,1)}, bf16[16,128,256]{2,1,0:T(8,128)(2,1)}, u32[]{:S(2)}, u32[]{:S(2)}) collective-permute-start(bf16[16,128,256]{2,1,0:T(8,128)(2,1)} %get-tuple-element.26), channel_id=1, source_target_pairs={{2,0},{4,2},{6,4},{8,6},{10,8},{12,10},{14,12},{16,14},{18,16},{20... | collective-permute-start | bytes 3145736 | tf_op jit(solution)/shard_map/ppermute | solution.py:170
  37.3 2.3 %copy-start.5 = (f32[4,128,256]{2,1,0:T(8,128)}, f32[4,128,256]{2,1,0:T(8,128)S(1)}, u32[]{:S(2)}) copy-start(f32[4,128,256]{2,1,0:T(8,128)S(1)} %get-tuple-element.20) | copy-start | bytes 1572868
  37.3 4.5 %collective-permute-start.2 = (f32[4,128,256]{2,1,0:T(8,128)}, f32[4,128,256]{2,1,0:T(8,128)}, u32[]{:S(2)}, u32[]{:S(2)}) collective-permute-start(f32[4,128,256]{2,1,0:T(8,128)} %get-tuple-element.21), channel_id=1, source_target_pairs={{0,1},{1,0},{2,3},{3,2},{4,5},{5,4},{6,7},{7,6},{8,9},{9,8},{10,11... | collective-permute-start | bytes 1572872 | tf_op jit(solution)/shard_map/ppermute | solution.py:174
  37.4 4.2 %copy-start.11 = (f32[32]{0:T(128)S(1)}, f32[32]{0:T(128)}, u32[]{:S(2)}) copy-start(f32[32]{0:T(128)} %param.17) | copy-start | bytes 388
  37.4 4.4 %copy-start.9 = (f32[16,256]{1,0:T(8,128)S(1)}, f32[16,256]{1,0:T(8,128)}, u32[]{:S(2)}) copy-start(f32[16,256]{1,0:T(8,128)} %param.16) | copy-start | bytes 49156
  39.0 2.5 %copy-start.6 = (f32[4,128,256]{2,1,0:T(8,128)}, f32[4,128,256]{2,1,0:T(8,128)S(1)}, u32[]{:S(2)}) copy-start(f32[4,128,256]{2,1,0:T(8,128)S(1)} %get-tuple-element.18) | copy-start | bytes 1572868
  39.0 4.1 %collective-permute-start.1 = (f32[4,128,256]{2,1,0:T(8,128)}, f32[4,128,256]{2,1,0:T(8,128)}, u32[]{:S(2)}, u32[]{:S(2)}) collective-permute-start(f32[4,128,256]{2,1,0:T(8,128)} %get-tuple-element.19), channel_id=1, source_target_pairs={{0,1},{1,0},{2,3},{3,2},{4,5},{5,4},{6,7},{7,6},{8,9},{9,8},{10,11... | collective-permute-start | bytes 1572872 | tf_op jit(solution)/shard_map/ppermute | solution.py:180
  39.6 46.8 %collective-permute-start.4 = (bf16[4,128,256]{2,1,0:T(8,128)(2,1)S(1)}, bf16[4,128,256]{2,1,0:T(8,128)(2,1)S(1)}, u32[]{:S(2)}, u32[]{:S(2)}) collective-permute-start(bf16[4,128,256]{2,1,0:T(8,128)(2,1)S(1)} %add_convert_fusion), channel_id=1, source_target_pairs={{2,0},{4,2},{6,4},{8,6},{10,8},{12,10},{14,12},{16,14},{18,16},{20... | collective-permute-start | bytes 786440 | tf_op jit(solution)/shard_map/ppermute | solution.py:178
  41.5 1.6 %copy-start.7 = (f32[4,128,256]{2,1,0:T(8,128)S(1)}, f32[4,128,256]{2,1,0:T(8,128)}, u32[]{:S(2)}) copy-start(f32[4,128,256]{2,1,0:T(8,128)} %copy-done.6) | copy-start | bytes 1572868
  86.5 1.6 %copy-start.4 = (bf16[16,256,256]{2,1,0:T(8,128)(2,1)S(1)}, bf16[16,256,256]{2,1,0:T(8,128)(2,1)}, u32[]{:S(2)}) copy-start(bf16[16,256,256]{2,1,0:T(8,128)(2,1)} %amps.3) | copy-start | bytes 6291460
  86.5 1.6 %copy-start.8 = (s32[16]{0:T(128)S(1)}, s32[16]{0:T(128)}, u32[]{:S(2)}) copy-start(s32[16]{0:T(128)} %counts.1) | copy-start | bytes 196

commit v2 on v1

--- a/solution.py
+++ b/solution.py
@@ -96,46 +96,79 @@
     )(core, left, right)
 
 
-def base_kernel(core, table, shift, counts, near, energy, amps, mid, low, high, out):
-    pair = pl.program_id(0)
-    rows, width = out.shape[1], out.shape[2]
+def base_kernel(core, table, shift, near, energy, amps, mid, out):
+    rows = out.shape[1]
+    group = out.shape[0]
     start = pl.multiple_of(core[0] * rows, rows)
-    across = energy[0, 0:1, :]
-    down = jnp.broadcast_to(energy[0, 0:1, pl.ds(start, rows)], (rows, rows)).T[:, 0:1]
-    denominator = down + across - shift[pair]
-    total = near[table[pair]] + denominator * amps[0].astype(jnp.float32)
-    total += mid[0] + low[0].astype(jnp.float32) + high[0].astype(jnp.float32)
-    row = lax.broadcasted_iota(jnp.int32, (rows, width), 0) + start
-    col = lax.broadcasted_iota(jnp.int32, (rows, width), 1)
-    inside = (row < counts[pair]) & (col < counts[pair])
-    out[0] = jnp.where(inside, total, 0.0)
-
-
-def assemble(core, table, shift, counts, near, energy, amps, mid, low, high):
+    for k in range(group):
+        pair = pl.program_id(0) * group + k
+        across = energy[k]
+        down = jnp.broadcast_to(energy[k, :, pl.ds(start, rows)], (rows, rows)).T[:, 0:1]
+        denominator = down + across - shift[pair]
+        slot = table[pair]
+        product = near[jnp.minimum(slot, near.shape[0] - 1)]
+        product = jnp.where(slot < near.shape[0], product, 0.0)
+        out[k] = product + denominator * amps[k].astype(jnp.float32) + mid[k]
+
+
+def base_sums(core, table, shift, near, energy, amps, mid, group):
     pairs, rows, width = mid.shape
-    one = pl.BlockSpec((1, rows, width), lambda p, *_: (p, 0, 0))
+    part = pl.BlockSpec((group, rows, width), lambda p, *_: (p, 0, 0))
     return pl.pallas_call(
         base_kernel,
         grid_spec=pltpu.PrefetchScalarGridSpec(
-            num_scalar_prefetch=4,
-            grid=(pairs,),
+            num_scalar_prefetch=3,
+            grid=(pairs // group,),
             in_specs=[
                 pl.BlockSpec(near.shape, lambda p, *_: (0, 0, 0)),
-                pl.BlockSpec((1, 1, width), lambda p, *_: (p, 0, 0)),
-                pl.BlockSpec((1, rows, width), lambda p, core, *_: (p, core[0], 0)),
-                one,
-                one,
-                one,
+                pl.BlockSpec((group, 1, width), lambda p, *_: (p, 0, 0)),
+                pl.BlockSpec((group, rows, width), lambda p, core, *_: (p, core[0], 0)),
+                part,
             ],
-            out_specs=one,
+            out_specs=part,
         ),
         out_shape=jax.ShapeDtypeStruct((pairs, rows, width), jnp.float32),
-        compiler_params=pltpu.CompilerParams(vmem_limit_bytes=24 * MIB),
-        cost_estimate=pl.CostEstimate(
-            flops=8 * mid.size, bytes_accessed=16 * mid.size, transcendentals=0
-        ),
-        name="assemble",
-    )(core, table, shift, counts, near, energy[:, None, :], amps, mid, low, high)
+        compiler_params=pltpu.CompilerParams(vmem_limit_bytes=16 * MIB),
+        cost_estimate=pl.CostEstimate(
+            flops=8 * mid.size, bytes_accessed=12 * mid.size, transcendentals=0
+        ),
+        name="base_sums",
+    )(core, table, shift, near, energy[:, None, :], amps, mid)
+
+
+def last_kernel(core, table, counts, above, base, low, high, out):
+    group, rows, width = out.shape
+    row = lax.broadcasted_iota(jnp.int32, (rows, width), 0) + core[0] * rows
+    col = lax.broadcasted_iota(jnp.int32, (rows, width), 1)
+    most = jnp.maximum(row, col)
+    near = 2 * above.shape[0]
+    for k in range(group):
+        pair = pl.program_id(0) * group + k
+        slot = table[pair] - near
+        product = above[jnp.maximum(slot, 0)].astype(jnp.float32)
+        total = base[k] + low[k].astype(jnp.float32) + high[k].astype(jnp.float32)
+        total += jnp.where(slot >= 0, product, 0.0)
+        out[k] = jnp.where(most < counts[pair], total, 0.0)
+
+
+def last_sums(core, table, counts, above, base, low, high, group):
+    pairs, rows, width = base.shape
+    part = pl.BlockSpec((group, rows, width), lambda p, *_: (p, 0, 0))
+    return pl.pallas_call(
+        last_kernel,
+        grid_spec=pltpu.PrefetchScalarGridSpec(
+            num_scalar_prefetch=3,
+            grid=(pairs // group,),
+            in_specs=[pl.BlockSpec(above.shape, lambda p, *_: (0, 0, 0)), part, part, part],
+            out_specs=part,
+        ),
+        out_shape=jax.ShapeDtypeStruct((pairs, rows, width), jnp.float32),
+        compiler_params=pltpu.CompilerParams(vmem_limit_bytes=16 * MIB),
+        cost_estimate=pl.CostEstimate(
+            flops=6 * base.size, bytes_accessed=12 * base.size, transcendentals=0
+        ),
+        name="last_sums",
+    )(core, table, counts, above, base, low, high)
 
 
 def local(
@@ -166,29 +199,30 @@
     slots = jnp.clip(slots - (holder - 1) * pairs, 0, 3 * pairs - 1)
     weights = lax.dynamic_slice_in_dim(couple_weight, holder * pairs, pairs, 0)
     low, mid, high = coupling_sums(where, slots, weights, margins, amplitudes, rows)
-    below, mid = lax.optimization_barrier((below, mid))
     from_upper = lax.ppermute(low, "pairs", down)
     from_lower = lax.ppermute(high, "pairs", up)
 
-    own_mine, own_other = products(where, blocks, blocks, rows)
+    own_blocks, mid = lax.optimization_barrier((blocks, mid))
+    own_mine, own_other = products(where, own_blocks, own_blocks, rows)
     own = own_mine + lax.ppermute(own_other, "aux", swap)
+    below, own = lax.optimization_barrier((below, own))
 
     back_mine, back_other = products(where, below, blocks, rows)
     back = (back_mine + lax.ppermute(back_other, "aux", swap)).astype(jnp.bfloat16)
-    above = lax.ppermute(back, "pairs", down).astype(jnp.float32)
+    above = lax.ppermute(back, "pairs", down)
     left_mine, left_other = products(where, blocks, below, rows)
     left = left_mine + lax.ppermute(left_other, "aux", swap)
 
-    near = jnp.concatenate([left, own, above], axis=0)
+    near = jnp.concatenate([left, own], axis=0)
     first = pair_orbs[:, 0] - holder * orbs
     second = pair_orbs[:, 1] - (holder - 1) * orbs
     table = (second // orbs) * (orbs * orbs) + first * orbs + second % orbs
     orbitals = jnp.arange(occ_energy.shape[0], dtype=jnp.int32)
     pick = lambda o: jnp.sum(jnp.where(o[:, None] == orbitals[None, :], occ_energy[None, :], 0.0), axis=1)
     shift = pick(pair_orbs[:, 0]) + pick(pair_orbs[:, 1])
-    return assemble(
-        where, table, shift, pno_count, near, pno_energy, amplitudes, mid, from_lower, from_upper
-    )
+    group = 4 if pairs % 4 == 0 else 1
+    base = base_sums(where, table, shift, near, pno_energy, amplitudes, mid, group)
+    return last_sums(where, table, pno_count, above, base, from_lower, from_upper, group)
 
 
 def solution(mesh):

time: 101 us -> 93.6 us (0.927)
  Pallas kernels: 25.9 us -> 21.6 us
  waiting for transfers between devices: 49.8 us -> 47 us
    ppermute x1, waiting for transfers between devices: 42.2 us -> 5.47 us  [local(): above = lax.ppermute(back, 'pairs', down)]
    ppermute x1, waiting for transfers between devices: 0.01 us -> 23 us  [local(): from_upper = lax.ppermute(low, 'pairs', down)]
    ppermute x1, waiting for transfers between devices: 0.01 us -> 12.8 us  [local(): from_lower = lax.ppermute(high, 'pairs', up)]
    pallas_call x1 -> x2, Pallas kernels: 10.9 us -> 6.49 us  [the longest x1 4.59 us: last_sums(): pl.pallas_call(last_kernel, grid_spec=pltpu.PrefetchScalarGridSpec(num_sc...]
    ppermute x1, waiting for transfers between devices: 7.54 us -> 3.85 us  [local(): below = lax.ppermute(blocks, 'pairs', up)]
    ppermute x1, waiting for transfers between devices: 0.01 us -> 1.9 us  [local(): own = own_mine + lax.ppermute(own_other, 'aux', swap)]
    convert_element_type x1, other arithmetic: 0.08 us -> 1.25 us  [local(): (back_mine + lax.ppermute(back_other, 'aux', swap)).astype(jnp.bfloat16)]
  transfers between devices with their start and end apart: 7 -> 7, of which waited for: 2 -> 5; matrix products, arithmetic and copies ran while one was open for 4% -> 5% of each run, Pallas kernels for 14% -> 17%
where the time goes in v2:
time: 93.6 us; the launch traced here: 92.5 us
  waiting for transfers between devices  47 us (50%)
  Pallas kernels  21.6 us (23%)
  starting transfers between devices  12.6 us (13%)
  local copies, waits for them, and re-layouts  7.62 us (8%)
  other arithmetic  3.56 us (4%)
    ppermute x1, waiting for transfers between devices, local(): from_upper = lax.ppermute(low, 'pairs', down)  23 us
    ppermute x1, waiting for transfers between devices, local(): from_lower = lax.ppermute(high, 'pairs', up)  12.8 us
    pallas_call x1, Pallas kernels, coupling_sums(): pl.pallas_call(term_kernel, grid_spec=pltpu.PrefetchScalarGridSpec(num_sc...  11 us
    unnamed x26, local copies, waits for them, and re-layouts  6.77 us
    ppermute x1, waiting for transfers between devices, local(): above = lax.ppermute(back, 'pairs', down)  5.47 us
    pallas_call x1, Pallas kernels, last_sums(): pl.pallas_call(last_kernel, grid_spec=pltpu.PrefetchScalarGridSpec(num_sc...  4.59 us
    ppermute x1, starting transfers between devices, local(): from_upper = lax.ppermute(low, 'pairs', down)  4.24 us
    pallas_call x3, Pallas kernels, products(): pl.pallas_call(product_kernel, in_specs=[pl.BlockSpec(memory_space=pltpu....  4.11 us
  transfers between devices with their start and end apart: 7, of which 5 were waited for; matrix products, arithmetic and copies ran while one was open for 5% of the time, Pallas kernels for 17%

profile of v2, /device:TPU:12, one launch (start us, length us, event | category | flops | bytes accessed | tf_op | source)
XLA Modules:
  0.0 92.5 jit_solution(14819772630362477104)
XLA Ops:
  0.0 3.5 %collective-permute-start = (bf16[2,1024,256]{2,1,0:T(8,128)(2,1)}, bf16[2,1024,256]{2,1,0:T(8,128)(2,1)S(1)}, u32[]{:S(2)}, u32[]{:S(2)}) collective-permute-start(bf16[2,1024,256]{2,1,0:T(8,128)(2,1)} %left.2), channel_id=1, source_target_pairs={{0,2},{2,4},{4,6},{6,8},{8,10},{10,12},{12,14},{14,16},{16,18},{18... | collective-permute-start | bytes 3145736 | tf_op jit(solution)/shard_map/ppermute | solution.py:196
  3.6 0.8 constant_dynamic-slice_fusion
  4.6 3.4 %copy-done.2 = bf16[16,4,256,256]{3,2,1,0:T(8,128)(2,1)S(1)} copy-done((bf16[16,4,256,256]{3,2,1,0:T(8,128)(2,1)S(1)}, bf16[16,4,256,256]{3,2,1,0:T(8,128)(2,1)}, u32[]{:S(2)}) %copy-start.2) | copy-done | bytes 8388632
  7.9 1.6 %copy-done.3 = bf16[16,256,256]{2,1,0:T(8,128)(2,1)S(1)} copy-done((bf16[16,256,256]{2,1,0:T(8,128)(2,1)S(1)}, bf16[16,256,256]{2,1,0:T(8,128)(2,1)}, u32[]{:S(2)}) %copy-start.3) | copy-done | bytes 2097176
  9.5 11.0 %coupling_sums.1 = (bf16[16,128,256]{2,1,0:T(8,128)(2,1)}, f32[16,128,256]{2,1,0:T(8,128)S(1)}, bf16[16,128,256]{2,1,0:T(8,128)(2,1)}) custom-call(s32[1]{0:T(128)} %bitcast.core, s32[16,4]{1,0:T(8,128)S(1)} %subtract_clamp_fusion.slots, f32[16,4]{1,0:T(8,128)S(1)} %copy.15.weights, bf16[16,4,256,256]{3,2,1,0:T(8,128)(2,1)S(1)} %copy-done.2, ...), custom_call_target="tpu_custom_call" | custom-call | flops 2147483648 | bytes 10485760 | tf_op jit(solution)/shard_map/coupling_sums/pallas_call | solution.py:41
  20.5 0.8 orbital_products.3
  21.4 1.9 %collective-permute-done.1 = f32[4,128,256]{2,1,0:T(8,128)S(1)} collective-permute-done((f32[4,128,256]{2,1,0:T(8,128)S(1)}, f32[4,128,256]{2,1,0:T(8,128)S(1)}, u32[]{:S(2)}, u32[]{:S(2)}) %collective-permute-start.1) | collective-permute-done | bytes 524320 | tf_op jit(solution)/shard_map/ppermute | solution.py:207
  23.3 0.9 add.34
  24.2 3.9 %collective-permute-done.left.right = bf16[2,1024,256]{2,1,0:T(8,128)(2,1)S(1)} collective-permute-done((bf16[2,1024,256]{2,1,0:T(8,128)(2,1)}, bf16[2,1024,256]{2,1,0:T(8,128)(2,1)S(1)}, u32[]{:S(2)}, u32[]{:S(2)}) %collective-permute-start) | collective-permute-done | bytes 1048608 | tf_op jit(solution)/shard_map/ppermute | solution.py:196
  28.0 1.6 %orbital_products.4 = (f32[4,128,256]{2,1,0:T(8,128)S(1)}, f32[4,128,256]{2,1,0:T(8,128)}) custom-call(s32[1]{0:T(128)} %bitcast.core, bf16[2,1024,256]{2,1,0:T(8,128)(2,1)S(1)} %collective-permute-done.left.right, bf16[2,1024,256]{2,1,0:T(8,128)(2,1)S(1)} %copy-done.1), custom_call_target="tpu_custom_call" | custom-call | flops 536870912 | bytes 3145728 | tf_op jit(solution)/shard_map/orbital_products/pallas_call | solution.py:83
  29.7 0.8 copy-done.6
  30.4 2.5 %collective-permute-start.5 = (bf16[16,128,256]{2,1,0:T(8,128)(2,1)}, bf16[16,128,256]{2,1,0:T(8,128)(2,1)}, u32[]{:S(2)}, u32[]{:S(2)}) collective-permute-start(bf16[16,128,256]{2,1,0:T(8,128)(2,1)} %get-tuple-element.29), channel_id=1, source_target_pairs={{0,2},{2,4},{4,6},{6,8},{8,10},{10,12},{12,14},{14,16},{16,18},{18... | collective-permute-start | bytes 3145736 | tf_op jit(solution)/shard_map/ppermute | solution.py:203
  32.9 4.2 %collective-permute-start.6 = (bf16[16,128,256]{2,1,0:T(8,128)(2,1)}, bf16[16,128,256]{2,1,0:T(8,128)(2,1)}, u32[]{:S(2)}, u32[]{:S(2)}) collective-permute-start(bf16[16,128,256]{2,1,0:T(8,128)(2,1)} %get-tuple-element.30), channel_id=1, source_target_pairs={{2,0},{4,2},{6,4},{8,6},{10,8},{12,10},{14,12},{16,14},{18,16},{20... | collective-permute-start | bytes 3145736 | tf_op jit(solution)/shard_map/ppermute | solution.py:202
  37.2 1.7 %orbital_products.5 = (f32[4,128,256]{2,1,0:T(8,128)S(1)}, f32[4,128,256]{2,1,0:T(8,128)}) custom-call(s32[1]{0:T(128)} %bitcast.core, bf16[2,1024,256]{2,1,0:T(8,128)(2,1)S(1)} %copy-done.1, bf16[2,1024,256]{2,1,0:T(8,128)(2,1)S(1)} %collective-permute-done.left.right), custom_call_target="tpu_custom_call" | custom-call | flops 536870912 | bytes 3145728 | tf_op jit(solution)/shard_map/orbital_products/pallas_call | solution.py:83
  38.9 0.8 copy-done.5
  39.7 0.2 select_reduce_fusion
  39.9 1.3 %add_convert_fusion = bf16[4,128,256]{2,1,0:T(8,128)(2,1)S(1)} fusion(f32[4,128,256]{2,1,0:T(8,128)} %copy-done.6, f32[4,128,256]{2,1,0:T(8,128)} %collective-permute-done.2), kind=kLoop, calls=%fused_computation.1 | loop fusion | flops 262144 | bytes 1310720 | tf_op jit(solution)/shard_map/convert_element_type | solution.py:211
  41.2 2.3 %collective-permute-start.3 = (bf16[4,128,256]{2,1,0:T(8,128)(2,1)S(1)}, bf16[4,128,256]{2,1,0:T(8,128)(2,1)S(1)}, u32[]{:S(2)}, u32[]{:S(2)}) collective-permute-start(bf16[4,128,256]{2,1,0:T(8,128)(2,1)S(1)} %add_convert_fusion), channel_id=1, source_target_pairs={{2,0},{4,2},{6,4},{8,6},{10,8},{12,10},{14,12},{16,14},{18,16},{20... | collective-permute-start | bytes 786440 | tf_op jit(solution)/shard_map/ppermute | solution.py:212
  43.5 1.1 %add.37 = f32[4,128,256]{2,1,0:T(8,128)S(1)} add(f32[4,128,256]{2,1,0:T(8,128)} %copy-done.5, f32[4,128,256]{2,1,0:T(8,128)S(1)} %collective-permute-done.4) | non-fusion elementwise | flops 131072 | bytes 1572864 | tf_op jit(solution)/shard_map/add | solution.py:214
  44.8 1.9 %base_sums.1.base = f32[16,128,256]{2,1,0:T(8,128)S(1)} custom-call(s32[1]{0:T(128)} %bitcast.core, s32[16]{0:T(128)S(1)} %fusion.table, f32[16]{0:T(128)S(1)} %add.36.shift, f32[8,128,256]{2,1,0:T(8,128)S(1)} %pad_maximum_fusion.near, f32[16,1,256]{2,1,0:T(1,128)S(1)} %broadcast_in_dim.25.energy, bf16[16,256,256]{2,1,0:T(8,128)(2,1)S(1)} %copy-done.4, ...), custom_call_target="tpu_custom_call" | custom-call | flops 4194304 | bytes 6291456 | tf_op jit(solution)/shard_map/base_sums/pallas_call | solution.py:117
  46.7 12.8 %collective-permute-done.5.low = bf16[16,128,256]{2,1,0:T(8,128)(2,1)} collective-permute-done((bf16[16,128,256]{2,1,0:T(8,128)(2,1)}, bf16[16,128,256]{2,1,0:T(8,128)(2,1)}, u32[]{:S(2)}, u32[]{:S(2)}) %collective-permute-start.5) | collective-permute-done | bytes 1048608 | tf_op jit(solution)/shard_map/ppermute | solution.py:203
  59.5 23.0 %collective-permute-done.6.high = bf16[16,128,256]{2,1,0:T(8,128)(2,1)} collective-permute-done((bf16[16,128,256]{2,1,0:T(8,128)(2,1)}, bf16[16,128,256]{2,1,0:T(8,128)(2,1)}, u32[]{:S(2)}, u32[]{:S(2)}) %collective-permute-start.6) | collective-permute-done | bytes 1048608 | tf_op jit(solution)/shard_map/ppermute | solution.py:202
  82.5 5.5 %collective-permute-done.3.above = bf16[4,128,256]{2,1,0:T(8,128)(2,1)S(1)} collective-permute-done((bf16[4,128,256]{2,1,0:T(8,128)(2,1)S(1)}, bf16[4,128,256]{2,1,0:T(8,128)(2,1)S(1)}, u32[]{:S(2)}, u32[]{:S(2)}) %collective-permute-start.3) | collective-permute-done | bytes 262176 | tf_op jit(solution)/shard_map/ppermute | solution.py:212
  87.9 4.6 %last_sums.1 = f32[16,128,256]{2,1,0:T(8,128)} custom-call(s32[1]{0:T(128)} %bitcast.core, s32[16]{0:T(128)S(1)} %fusion.table, s32[16]{0:T(128)S(1)} %copy-done.7, bf16[4,128,256]{2,1,0:T(8,128)(2,1)S(1)} %collective-permute-done.3.above, f32[16,128,256]{2,1,0:T(8,128)S(1)} %base_sums.1.base, bf16[16,128,256]{2,1,0:T(8,128)(2,1)} %collective-permute-done.5.low, ...), custom_call_target="tpu_custom_call" | custom-call | flops 3145728 | bytes 6291456 | tf_op jit(solution)/shard_map/last_sums/pallas_call | solution.py:157
  (34 shorter events, 0.5 us)
Async XLA Ops:
  0.0 3.5 %copy-start = (s32[256,4]{0,1:T(4,128)S(1)}, s32[256,4]{0,1:T(4,128)}, u32[]{:S(2)}) copy-start(s32[256,4]{0,1:T(4,128)} %param.14) | copy-start | bytes 12292
  0.0 28.0 %collective-permute-start = (bf16[2,1024,256]{2,1,0:T(8,128)(2,1)}, bf16[2,1024,256]{2,1,0:T(8,128)(2,1)S(1)}, u32[]{:S(2)}, u32[]{:S(2)}) collective-permute-start(bf16[2,1024,256]{2,1,0:T(8,128)(2,1)} %left.2), channel_id=1, source_target_pairs={{0,2},{2,4},{4,6},{6,8},{8,10},{10,12},{12,14},{14,16},{16,18},{18... | collective-permute-start | bytes 3145736 | tf_op jit(solution)/shard_map/ppermute | solution.py:196
  4.5 3.4 %copy-start.2 = (bf16[16,4,256,256]{3,2,1,0:T(8,128)(2,1)S(1)}, bf16[16,4,256,256]{3,2,1,0:T(8,128)(2,1)}, u32[]{:S(2)}) copy-start(bf16[16,4,256,256]{3,2,1,0:T(8,128)(2,1)} %margins.1) | copy-start | bytes 25165828
  7.9 1.6 %copy-start.3 = (bf16[16,256,256]{2,1,0:T(8,128)(2,1)S(1)}, bf16[16,256,256]{2,1,0:T(8,128)(2,1)}, u32[]{:S(2)}) copy-start(bf16[16,256,256]{2,1,0:T(8,128)(2,1)} %amps.3) | copy-start | bytes 6291460
  9.5 11.0 %copy-start.1 = (bf16[2,1024,256]{2,1,0:T(8,128)(2,1)S(1)}, bf16[2,1024,256]{2,1,0:T(8,128)(2,1)}, u32[]{:S(2)}) copy-start(bf16[2,1024,256]{2,1,0:T(8,128)(2,1)} %left.2) | copy-start | bytes 3145732
  21.3 15.9 %copy-start.10 = (s32[16,2]{0,1:T(2,128)S(1)}, s32[16,2]{0,1:T(2,128)}, u32[]{:S(2)}) copy-start(s32[16,2]{0,1:T(2,128)} %param.10) | copy-start | bytes 388
  21.3 2.0 %collective-permute-start.1 = (f32[4,128,256]{2,1,0:T(8,128)S(1)}, f32[4,128,256]{2,1,0:T(8,128)S(1)}, u32[]{:S(2)}, u32[]{:S(2)}) collective-permute-start(f32[4,128,256]{2,1,0:T(8,128)S(1)} %get-tuple-element.21), channel_id=1, source_target_pairs={{0,1},{1,0},{2,3},{3,2},{4,5},{5,4},{6,7},{7,6},{8,9},{9,8},{10,11... | collective-permute-start | bytes 1572872 | tf_op jit(solution)/shard_map/ppermute | solution.py:207
  24.2 15.5 %copy-start.11 = (f32[32]{0:T(128)S(1)}, f32[32]{0:T(128)}, u32[]{:S(2)}) copy-start(f32[32]{0:T(128)} %param.17) | copy-start | bytes 388
  24.2 15.7 %copy-start.9 = (f32[16,256]{1,0:T(8,128)S(1)}, f32[16,256]{1,0:T(8,128)}, u32[]{:S(2)}) copy-start(f32[16,256]{1,0:T(8,128)} %param.16) | copy-start | bytes 49156
  29.7 0.8 copy-start.6
  30.4 9.5 %collective-permute-start.2 = (f32[4,128,256]{2,1,0:T(8,128)}, f32[4,128,256]{2,1,0:T(8,128)}, u32[]{:S(2)}, u32[]{:S(2)}) collective-permute-start(f32[4,128,256]{2,1,0:T(8,128)} %get-tuple-element.24), channel_id=1, source_target_pairs={{0,1},{1,0},{2,3},{3,2},{4,5},{5,4},{6,7},{7,6},{8,9},{9,8},{10,11... | collective-permute-start | bytes 1572872 | tf_op jit(solution)/shard_map/ppermute | solution.py:211
  30.4 29.1 %collective-permute-start.5 = (bf16[16,128,256]{2,1,0:T(8,128)(2,1)}, bf16[16,128,256]{2,1,0:T(8,128)(2,1)}, u32[]{:S(2)}, u32[]{:S(2)}) collective-permute-start(bf16[16,128,256]{2,1,0:T(8,128)(2,1)} %get-tuple-element.29), channel_id=1, source_target_pairs={{0,2},{2,4},{4,6},{6,8},{8,10},{10,12},{12,14},{14,16},{16,18},{18... | collective-permute-start | bytes 3145736 | tf_op jit(solution)/shard_map/ppermute | solution.py:203
  32.9 49.5 %collective-permute-start.6 = (bf16[16,128,256]{2,1,0:T(8,128)(2,1)}, bf16[16,128,256]{2,1,0:T(8,128)(2,1)}, u32[]{:S(2)}, u32[]{:S(2)}) collective-permute-start(bf16[16,128,256]{2,1,0:T(8,128)(2,1)} %get-tuple-element.30), channel_id=1, source_target_pairs={{2,0},{4,2},{6,4},{8,6},{10,8},{12,10},{14,12},{16,14},{18,16},{20... | collective-permute-start | bytes 3145736 | tf_op jit(solution)/shard_map/ppermute | solution.py:202
  38.9 0.8 copy-start.5
  39.7 5.0 %copy-start.8 = (f32[4,128,256]{2,1,0:T(8,128)S(1)}, f32[4,128,256]{2,1,0:T(8,128)}, u32[]{:S(2)}) copy-start(f32[4,128,256]{2,1,0:T(8,128)} %add.34) | copy-start | bytes 1572868
  39.7 3.8 %collective-permute-start.4 = (f32[4,128,256]{2,1,0:T(8,128)}, f32[4,128,256]{2,1,0:T(8,128)S(1)}, u32[]{:S(2)}, u32[]{:S(2)}) collective-permute-start(f32[4,128,256]{2,1,0:T(8,128)} %get-tuple-element.26), channel_id=1, source_target_pairs={{0,1},{1,0},{2,3},{3,2},{4,5},{5,4},{6,7},{7,6},{8,9},{9,8},{10,11... | collective-permute-start | bytes 1572872 | tf_op jit(solution)/shard_map/ppermute | solution.py:214
  41.2 3.6 %copy-start.4 = (bf16[16,256,256]{2,1,0:T(8,128)(2,1)S(1)}, bf16[16,256,256]{2,1,0:T(8,128)(2,1)}, u32[]{:S(2)}) copy-start(bf16[16,256,256]{2,1,0:T(8,128)(2,1)} %amps.3) | copy-start | bytes 6291460
  41.2 46.7 %collective-permute-start.3 = (bf16[4,128,256]{2,1,0:T(8,128)(2,1)S(1)}, bf16[4,128,256]{2,1,0:T(8,128)(2,1)S(1)}, u32[]{:S(2)}, u32[]{:S(2)}) collective-permute-start(bf16[4,128,256]{2,1,0:T(8,128)(2,1)S(1)} %add_convert_fusion), channel_id=1, source_target_pairs={{2,0},{4,2},{6,4},{8,6},{10,8},{12,10},{14,12},{16,14},{18,16},{20... | collective-permute-start | bytes 786440 | tf_op jit(solution)/shard_map/ppermute | solution.py:212
  44.8 43.2 %copy-start.7 = (s32[16]{0:T(128)S(1)}, s32[16]{0:T(128)}, u32[]{:S(2)}) copy-start(s32[16]{0:T(128)} %counts.1) | copy-start | bytes 196

commit v3 on v2

--- a/solution.py
+++ b/solution.py
@@ -55,7 +55,7 @@
             jax.ShapeDtypeStruct((pairs, rows, width), jnp.float32),
             jax.ShapeDtypeStruct((pairs, rows, width), jnp.bfloat16),
         ],
-        compiler_params=pltpu.CompilerParams(vmem_limit_bytes=32 * MIB),
+        compiler_params=pltpu.CompilerParams(vmem_limit_bytes=52 * MIB),
         cost_estimate=pl.CostEstimate(
             flops=flops, bytes_accessed=2 * margins.size + 2 * amps.size, transcendentals=0
         ),
@@ -88,8 +88,8 @@
         scratch_shapes=[pltpu.VMEM((count, width, width), jnp.float32)],
         compiler_params=pltpu.CompilerParams(vmem_limit_bytes=24 * MIB),
         cost_estimate=pl.CostEstimate(
-            flops=2 * count * left.shape[1] * width * width,
-            bytes_accessed=4 * left.size + 8 * count * rows * width,
+            flops=count * width,
+            bytes_accessed=count * width,
             transcendentals=0,
         ),
         name="orbital_products",
@@ -130,7 +130,7 @@
         out_shape=jax.ShapeDtypeStruct((pairs, rows, width), jnp.float32),
         compiler_params=pltpu.CompilerParams(vmem_limit_bytes=16 * MIB),
         cost_estimate=pl.CostEstimate(
-            flops=8 * mid.size, bytes_accessed=12 * mid.size, transcendentals=0
+            flops=mid.size // 64, bytes_accessed=mid.size // 64, transcendentals=0
         ),
         name="base_sums",
     )(core, table, shift, near, energy[:, None, :], amps, mid)
@@ -205,7 +205,7 @@
     own_blocks, mid = lax.optimization_barrier((blocks, mid))
     own_mine, own_other = products(where, own_blocks, own_blocks, rows)
     own = own_mine + lax.ppermute(own_other, "aux", swap)
-    below, own = lax.optimization_barrier((below, own))
+    below, own, from_upper = lax.optimization_barrier((below, own, from_upper))
 
     back_mine, back_other = products(where, below, blocks, rows)
     back = (back_mine + lax.ppermute(back_other, "aux", swap)).astype(jnp.bfloat16)

time: 93.6 us -> 90.7 us (0.969)
  local copies, waits for them, and re-layouts: 7.62 us -> 2.66 us
  Pallas kernels: 21.6 us -> 25.3 us
  waiting for transfers between devices: 47 us -> 43.8 us
  starting transfers between devices: 12.6 us -> 14 us
    pallas_call x1, Pallas kernels: 11 us -> 16.6 us  [coupling_sums(): pl.pallas_call(term_kernel, grid_spec=pltpu.PrefetchScalarGridSpec(num_sc...]
    unnamed x26 -> x24, local copies, waits for them, and re-layouts: 6.77 us -> 1.82 us
    ppermute x1, waiting for transfers between devices: 3.85 us -> 0.96 us  [local(): below = lax.ppermute(blocks, 'pairs', up)]
    ppermute x1, starting transfers between devices: 2.27 us -> 4.37 us  [local(): above = lax.ppermute(back, 'pairs', down)]
    pallas_call x1, Pallas kernels: 4.59 us -> 2.68 us  [last_sums(): pl.pallas_call(last_kernel, grid_spec=pltpu.PrefetchScalarGridSpec(num_sc...]
    ppermute x1, waiting for transfers between devices: 23 us -> 21.3 us  [local(): from_upper = lax.ppermute(low, 'pairs', down)]
    ppermute x1, waiting for transfers between devices: 12.8 us -> 14.4 us  [local(): from_lower = lax.ppermute(high, 'pairs', up)]
  transfers between devices with their start and end apart: 7 -> 7, of which waited for: 5 -> 5; matrix products, arithmetic and copies ran while one was open for 5% -> 5% of each run, Pallas kernels for 17% -> 23%
where the time goes in v3:
time: 90.7 us; the launch traced here: 89.8 us
  waiting for transfers between devices  43.8 us (48%)
  Pallas kernels  25.3 us (28%)
  starting transfers between devices  14 us (15%)
  other arithmetic  3.87 us (4%)
  local copies, waits for them, and re-layouts  2.66 us (3%)
    ppermute x1, waiting for transfers between devices, local(): from_upper = lax.ppermute(low, 'pairs', down)  21.3 us
    pallas_call x1, Pallas kernels, coupling_sums(): pl.pallas_call(term_kernel, grid_spec=pltpu.PrefetchScalarGridSpec(num_sc...  16.6 us
    ppermute x1, waiting for transfers between devices, local(): from_lower = lax.ppermute(high, 'pairs', up)  14.4 us
    ppermute x1, waiting for transfers between devices, local(): above = lax.ppermute(back, 'pairs', down)  5.28 us
    ppermute x1, starting transfers between devices, local(): above = lax.ppermute(back, 'pairs', down)  4.37 us
    pallas_call x3, Pallas kernels, products(): pl.pallas_call(product_kernel, in_specs=[pl.BlockSpec(memory_space=pltpu....  4.1 us
    ppermute x1, starting transfers between devices, local(): below = lax.ppermute(blocks, 'pairs', up)  3.52 us
    ppermute x1, starting transfers between devices, local(): from_upper = lax.ppermute(low, 'pairs', down)  3.33 us
  transfers between devices with their start and end apart: 7, of which 5 were waited for; matrix products, arithmetic and copies ran while one was open for 5% of the time, Pallas kernels for 23%

profile of v3, /device:TPU:12, one launch (start us, length us, event | category | flops | bytes accessed | tf_op | source)
XLA Modules:
  0.0 89.8 jit_solution(15642209574270133627)
XLA Ops:
  0.0 3.5 %collective-permute-start = (bf16[2,1024,256]{2,1,0:T(8,128)(2,1)}, bf16[2,1024,256]{2,1,0:T(8,128)(2,1)S(1)}, u32[]{:S(2)}, u32[]{:S(2)}) collective-permute-start(bf16[2,1024,256]{2,1,0:T(8,128)(2,1)} %left.2), channel_id=1, source_target_pairs={{0,2},{2,4},{4,6},{6,8},{8,10},{10,12},{12,14},{14,16},{16,18},{18... | collective-permute-start | bytes 3145736 | tf_op jit(solution)/shard_map/ppermute | solution.py:196
  3.7 0.8 constant_dynamic-slice_fusion
  4.6 16.6 %coupling_sums.1 = (bf16[16,128,256]{2,1,0:T(8,128)(2,1)S(1)}, f32[16,128,256]{2,1,0:T(8,128)}, bf16[16,128,256]{2,1,0:T(8,128)(2,1)}) custom-call(s32[1]{0:T(128)} %bitcast.core, s32[16,4]{1,0:T(8,128)S(1)} %subtract_clamp_fusion.slots, f32[16,4]{1,0:T(8,128)S(1)} %copy.15.weights, bf16[16,4,256,256]{3,2,1,0:T(8,128)(2,1)} %margins.1, ...), custom_call_target="tpu_custom_call" | custom-call | flops 2147483648 | bytes 10485760 | tf_op jit(solution)/shard_map/coupling_sums/pallas_call | solution.py:41
  21.2 3.3 %collective-permute-start.2 = (bf16[16,128,256]{2,1,0:T(8,128)(2,1)S(1)}, bf16[16,128,256]{2,1,0:T(8,128)(2,1)S(1)}, u32[]{:S(2)}, u32[]{:S(2)}) collective-permute-start(bf16[16,128,256]{2,1,0:T(8,128)(2,1)S(1)} %get-tuple-element.23), channel_id=1, source_target_pairs={{2,0},{4,2},{6,4},{8,6},{10,8},{12,10},{14,12},{16,14},{18,16},{20... | collective-permute-start | bytes 3145736 | tf_op jit(solution)/shard_map/ppermute | solution.py:202
  24.5 0.8 orbital_products.3
  25.4 1.9 %collective-permute-done.1 = f32[4,128,256]{2,1,0:T(8,128)S(1)} collective-permute-done((f32[4,128,256]{2,1,0:T(8,128)S(1)}, f32[4,128,256]{2,1,0:T(8,128)S(1)}, u32[]{:S(2)}, u32[]{:S(2)}) %collective-permute-start.1) | collective-permute-done | bytes 524320 | tf_op jit(solution)/shard_map/ppermute | solution.py:207
  27.3 0.9 add.34
  28.2 1.0 %collective-permute-done.left.right = bf16[2,1024,256]{2,1,0:T(8,128)(2,1)S(1)} collective-permute-done((bf16[2,1024,256]{2,1,0:T(8,128)(2,1)}, bf16[2,1024,256]{2,1,0:T(8,128)(2,1)S(1)}, u32[]{:S(2)}, u32[]{:S(2)}) %collective-permute-start) | collective-permute-done | bytes 1048608 | tf_op jit(solution)/shard_map/ppermute | solution.py:196
  29.2 21.3 %collective-permute-done.2.high = bf16[16,128,256]{2,1,0:T(8,128)(2,1)S(1)} collective-permute-done((bf16[16,128,256]{2,1,0:T(8,128)(2,1)S(1)}, bf16[16,128,256]{2,1,0:T(8,128)(2,1)S(1)}, u32[]{:S(2)}, u32[]{:S(2)}) %collective-permute-start.2) | collective-permute-done | bytes 1048608 | tf_op jit(solution)/shard_map/ppermute | solution.py:202
  50.4 1.6 %orbital_products.4 = (f32[4,128,256]{2,1,0:T(8,128)S(1)}, f32[4,128,256]{2,1,0:T(8,128)}) custom-call(s32[1]{0:T(128)} %bitcast.core, bf16[2,1024,256]{2,1,0:T(8,128)(2,1)S(1)} %collective-permute-done.left.right, bf16[2,1024,256]{2,1,0:T(8,128)(2,1)S(1)} %copy-done.1), custom_call_target="tpu_custom_call" | custom-call | flops 1024 | bytes 1024 | tf_op jit(solution)/shard_map/orbital_products/pallas_call | solution.py:83
  52.1 0.8 copy-done.5
  52.9 2.5 %collective-permute-start.6 = (bf16[16,128,256]{2,1,0:T(8,128)(2,1)}, bf16[16,128,256]{2,1,0:T(8,128)(2,1)S(1)}, u32[]{:S(2)}, u32[]{:S(2)}) collective-permute-start(bf16[16,128,256]{2,1,0:T(8,128)(2,1)} %get-tuple-element.31), channel_id=1, source_target_pairs={{0,2},{2,4},{4,6},{6,8},{8,10},{10,12},{12,14},{14,16},{16,18},{18... | collective-permute-start | bytes 3145736 | tf_op jit(solution)/shard_map/ppermute | solution.py:203
  55.4 1.6 %orbital_products.5 = (f32[4,128,256]{2,1,0:T(8,128)S(1)}, f32[4,128,256]{2,1,0:T(8,128)}) custom-call(s32[1]{0:T(128)} %bitcast.core, bf16[2,1024,256]{2,1,0:T(8,128)(2,1)S(1)} %copy-done.1, bf16[2,1024,256]{2,1,0:T(8,128)(2,1)S(1)} %collective-permute-done.left.right), custom_call_target="tpu_custom_call" | custom-call | flops 1024 | bytes 1024 | tf_op jit(solution)/shard_map/orbital_products/pallas_call | solution.py:83
  57.0 0.8 copy-done.4
  57.8 0.2 collective-permute-start.5
  58.1 0.2 select_reduce_fusion
  58.3 1.4 %add_convert_fusion = bf16[4,128,256]{2,1,0:T(8,128)(2,1)S(1)} fusion(f32[4,128,256]{2,1,0:T(8,128)} %copy-done.5, f32[4,128,256]{2,1,0:T(8,128)} %collective-permute-done.3), kind=kLoop, calls=%fused_computation.1 | loop fusion | flops 262144 | bytes 1310720 | tf_op jit(solution)/shard_map/convert_element_type | solution.py:211
  59.7 4.4 %collective-permute-start.4 = (bf16[4,128,256]{2,1,0:T(8,128)(2,1)S(1)}, bf16[4,128,256]{2,1,0:T(8,128)(2,1)S(1)}, u32[]{:S(2)}, u32[]{:S(2)}) collective-permute-start(bf16[4,128,256]{2,1,0:T(8,128)(2,1)S(1)} %add_convert_fusion), channel_id=1, source_target_pairs={{2,0},{4,2},{6,4},{8,6},{10,8},{12,10},{14,12},{16,14},{18,16},{20... | collective-permute-start | bytes 786440 | tf_op jit(solution)/shard_map/ppermute | solution.py:212
  64.1 1.3 %add.37 = f32[4,128,256]{2,1,0:T(8,128)S(1)} add(f32[4,128,256]{2,1,0:T(8,128)} %copy-done.4, f32[4,128,256]{2,1,0:T(8,128)} %collective-permute-done.5) | non-fusion elementwise | flops 131072 | bytes 1572864 | tf_op jit(solution)/shard_map/add | solution.py:214
  65.4 0.1 pad_maximum_fusion.near
  65.6 1.9 %base_sums.1.base = f32[16,128,256]{2,1,0:T(8,128)S(1)} custom-call(s32[1]{0:T(128)} %bitcast.core, s32[16]{0:T(128)S(1)} %fusion.table, f32[16]{0:T(128)S(1)} %add.36.shift, f32[8,128,256]{2,1,0:T(8,128)S(1)} %pad_maximum_fusion.near, f32[16,1,256]{2,1,0:T(1,128)S(1)} %broadcast_in_dim.25.energy, bf16[16,256,256]{2,1,0:T(8,128)(2,1)S(1)} %copy-done.2, ...), custom_call_target="tpu_custom_call" | custom-call | flops 8192 | bytes 8192 | tf_op jit(solution)/shard_map/base_sums/pallas_call | solution.py:117
  67.5 14.4 %collective-permute-done.6.low = bf16[16,128,256]{2,1,0:T(8,128)(2,1)S(1)} collective-permute-done((bf16[16,128,256]{2,1,0:T(8,128)(2,1)}, bf16[16,128,256]{2,1,0:T(8,128)(2,1)S(1)}, u32[]{:S(2)}, u32[]{:S(2)}) %collective-permute-start.6) | collective-permute-done | bytes 1048608 | tf_op jit(solution)/shard_map/ppermute | solution.py:203
  81.8 5.3 %collective-permute-done.4.above = bf16[4,128,256]{2,1,0:T(8,128)(2,1)S(1)} collective-permute-done((bf16[4,128,256]{2,1,0:T(8,128)(2,1)S(1)}, bf16[4,128,256]{2,1,0:T(8,128)(2,1)S(1)}, u32[]{:S(2)}, u32[]{:S(2)}) %collective-permute-start.4) | collective-permute-done | bytes 262176 | tf_op jit(solution)/shard_map/ppermute | solution.py:212
  87.1 2.7 %last_sums.1 = f32[16,128,256]{2,1,0:T(8,128)} custom-call(s32[1]{0:T(128)} %bitcast.core, s32[16]{0:T(128)S(1)} %fusion.table, s32[16]{0:T(128)S(1)} %copy-done.6, bf16[4,128,256]{2,1,0:T(8,128)(2,1)S(1)} %collective-permute-done.4.above, f32[16,128,256]{2,1,0:T(8,128)S(1)} %base_sums.1.base, bf16[16,128,256]{2,1,0:T(8,128)(2,1)S(1)} %collective-permute-done.6.low, ...), custom_call_target="tpu_custom_call" | custom-call | flops 3145728 | bytes 6291456 | tf_op jit(solution)/shard_map/last_sums/pallas_call | solution.py:157
  (32 shorter events, 0.4 us)
Async XLA Ops:
  0.0 3.5 %copy-start = (s32[256,4]{0,1:T(4,128)S(1)}, s32[256,4]{0,1:T(4,128)}, u32[]{:S(2)}) copy-start(s32[256,4]{0,1:T(4,128)} %param.14) | copy-start | bytes 12292
  0.0 29.2 %collective-permute-start = (bf16[2,1024,256]{2,1,0:T(8,128)(2,1)}, bf16[2,1024,256]{2,1,0:T(8,128)(2,1)S(1)}, u32[]{:S(2)}, u32[]{:S(2)}) collective-permute-start(bf16[2,1024,256]{2,1,0:T(8,128)(2,1)} %left.2), channel_id=1, source_target_pairs={{0,2},{2,4},{4,6},{6,8},{8,10},{10,12},{12,14},{14,16},{16,18},{18... | collective-permute-start | bytes 3145736 | tf_op jit(solution)/shard_map/ppermute | solution.py:196
  4.6 19.9 %copy-start.1 = (bf16[2,1024,256]{2,1,0:T(8,128)(2,1)S(1)}, bf16[2,1024,256]{2,1,0:T(8,128)(2,1)}, u32[]{:S(2)}) copy-start(bf16[2,1024,256]{2,1,0:T(8,128)(2,1)} %left.2) | copy-start | bytes 3145732
  21.2 29.3 %collective-permute-start.2 = (bf16[16,128,256]{2,1,0:T(8,128)(2,1)S(1)}, bf16[16,128,256]{2,1,0:T(8,128)(2,1)S(1)}, u32[]{:S(2)}, u32[]{:S(2)}) collective-permute-start(bf16[16,128,256]{2,1,0:T(8,128)(2,1)S(1)} %get-tuple-element.23), channel_id=1, source_target_pairs={{2,0},{4,2},{6,4},{8,6},{10,8},{12,10},{14,12},{16,14},{18,16},{20... | collective-permute-start | bytes 3145736 | tf_op jit(solution)/shard_map/ppermute | solution.py:202
  25.3 30.1 %copy-start.9 = (s32[16,2]{0,1:T(2,128)S(1)}, s32[16,2]{0,1:T(2,128)}, u32[]{:S(2)}) copy-start(s32[16,2]{0,1:T(2,128)} %param.10) | copy-start | bytes 388
  25.3 2.0 %collective-permute-start.1 = (f32[4,128,256]{2,1,0:T(8,128)S(1)}, f32[4,128,256]{2,1,0:T(8,128)S(1)}, u32[]{:S(2)}, u32[]{:S(2)}) collective-permute-start(f32[4,128,256]{2,1,0:T(8,128)S(1)} %get-tuple-element.22), channel_id=1, source_target_pairs={{0,1},{1,0},{2,3},{3,2},{4,5},{5,4},{6,7},{7,6},{8,9},{9,8},{10,11... | collective-permute-start | bytes 1572872 | tf_op jit(solution)/shard_map/ppermute | solution.py:207
  28.2 29.9 %copy-start.10 = (f32[32]{0:T(128)S(1)}, f32[32]{0:T(128)}, u32[]{:S(2)}) copy-start(f32[32]{0:T(128)} %param.17) | copy-start | bytes 388
  28.2 30.0 %copy-start.8 = (f32[16,256]{1,0:T(8,128)S(1)}, f32[16,256]{1,0:T(8,128)}, u32[]{:S(2)}) copy-start(f32[16,256]{1,0:T(8,128)} %param.16) | copy-start | bytes 49156
  52.1 0.8 copy-start.5
  52.9 5.4 %collective-permute-start.3 = (f32[4,128,256]{2,1,0:T(8,128)}, f32[4,128,256]{2,1,0:T(8,128)}, u32[]{:S(2)}, u32[]{:S(2)}) collective-permute-start(f32[4,128,256]{2,1,0:T(8,128)} %get-tuple-element.26), channel_id=1, source_target_pairs={{0,1},{1,0},{2,3},{3,2},{4,5},{5,4},{6,7},{7,6},{8,9},{9,8},{10,11... | collective-permute-start | bytes 1572872 | tf_op jit(solution)/shard_map/ppermute | solution.py:211
  52.9 28.9 %collective-permute-start.6 = (bf16[16,128,256]{2,1,0:T(8,128)(2,1)}, bf16[16,128,256]{2,1,0:T(8,128)(2,1)S(1)}, u32[]{:S(2)}, u32[]{:S(2)}) collective-permute-start(bf16[16,128,256]{2,1,0:T(8,128)(2,1)} %get-tuple-element.31), channel_id=1, source_target_pairs={{0,2},{2,4},{4,6},{6,8},{8,10},{10,12},{12,14},{14,16},{16,18},{18... | collective-permute-start | bytes 3145736 | tf_op jit(solution)/shard_map/ppermute | solution.py:203
  57.0 0.8 copy-start.4
  57.8 7.6 %copy-start.7 = (f32[4,128,256]{2,1,0:T(8,128)S(1)}, f32[4,128,256]{2,1,0:T(8,128)}, u32[]{:S(2)}) copy-start(f32[4,128,256]{2,1,0:T(8,128)} %add.34) | copy-start | bytes 1572868
  57.8 6.3 %collective-permute-start.5 = (f32[4,128,256]{2,1,0:T(8,128)}, f32[4,128,256]{2,1,0:T(8,128)}, u32[]{:S(2)}, u32[]{:S(2)}) collective-permute-start(f32[4,128,256]{2,1,0:T(8,128)} %get-tuple-element.28), channel_id=1, source_target_pairs={{0,1},{1,0},{2,3},{3,2},{4,5},{5,4},{6,7},{7,6},{8,9},{9,8},{10,11... | collective-permute-start | bytes 1572872 | tf_op jit(solution)/shard_map/ppermute | solution.py:214
  58.3 7.2 %copy-start.3 = (f32[16,128,256]{2,1,0:T(8,128)S(1)}, f32[16,128,256]{2,1,0:T(8,128)}, u32[]{:S(2)}) copy-start(f32[16,128,256]{2,1,0:T(8,128)} %get-tuple-element.30.mid) | copy-start | bytes 6291460
  59.7 5.8 %copy-start.2 = (bf16[16,256,256]{2,1,0:T(8,128)(2,1)S(1)}, bf16[16,256,256]{2,1,0:T(8,128)(2,1)}, u32[]{:S(2)}) copy-start(bf16[16,256,256]{2,1,0:T(8,128)(2,1)} %amps.3) | copy-start | bytes 6291460
  59.7 27.4 %collective-permute-start.4 = (bf16[4,128,256]{2,1,0:T(8,128)(2,1)S(1)}, bf16[4,128,256]{2,1,0:T(8,128)(2,1)S(1)}, u32[]{:S(2)}, u32[]{:S(2)}) collective-permute-start(bf16[4,128,256]{2,1,0:T(8,128)(2,1)S(1)} %add_convert_fusion), channel_id=1, source_target_pairs={{2,0},{4,2},{6,4},{8,6},{10,8},{12,10},{14,12},{16,14},{18,16},{20... | collective-permute-start | bytes 786440 | tf_op jit(solution)/shard_map/ppermute | solution.py:212
  65.6 21.6 %copy-start.6 = (s32[16]{0:T(128)S(1)}, s32[16]{0:T(128)}, u32[]{:S(2)}) copy-start(s32[16]{0:T(128)} %counts.1) | copy-start | bytes 196

commit v4 on v3

--- a/solution.py
+++ b/solution.py
@@ -205,13 +205,14 @@
     own_blocks, mid = lax.optimization_barrier((blocks, mid))
     own_mine, own_other = products(where, own_blocks, own_blocks, rows)
     own = own_mine + lax.ppermute(own_other, "aux", swap)
-    below, own, from_upper = lax.optimization_barrier((below, own, from_upper))
+    below, own = lax.optimization_barrier((below, own))
 
     back_mine, back_other = products(where, below, blocks, rows)
     back = (back_mine + lax.ppermute(back_other, "aux", swap)).astype(jnp.bfloat16)
-    above = lax.ppermute(back, "pairs", down)
     left_mine, left_other = products(where, blocks, below, rows)
     left = left_mine + lax.ppermute(left_other, "aux", swap)
+    back, left, from_upper = lax.optimization_barrier((back, left, from_upper))
+    above = lax.ppermute(back, "pairs", down)
 
     near = jnp.concatenate([left, own], axis=0)
     first = pair_orbs[:, 0] - holder * orbs

time: 90.7 us -> 86.2 us (0.950)
  starting transfers between devices: 14 us -> 11.4 us
  local copies, waits for them, and re-layouts: 2.66 us -> 1.06 us
    ppermute x1, waiting for transfers between devices: 21.3 us -> 35.8 us  [local(): from_upper = lax.ppermute(low, 'pairs', down)]
    ppermute x1, waiting for transfers between devices: 14.4 us -> 0.01 us  [local(): from_lower = lax.ppermute(high, 'pairs', up)]
    ppermute x1, starting transfers between devices: 4.37 us -> 1.91 us  [local(): above = lax.ppermute(back, 'pairs', down)]
    ppermute x1, waiting for transfers between devices: 1.9 us -> 0.01 us  [local(): own = own_mine + lax.ppermute(own_other, 'aux', swap)]
    unnamed x24 -> x20, local copies, waits for them, and re-layouts: 1.82 us -> 0.21 us
  transfers between devices with their start and end apart: 7 -> 7, of which waited for: 5 -> 3; matrix products, arithmetic and copies ran while one was open for 5% -> 6% of each run, Pallas kernels for 23% -> 27%
where the time goes in v4:
time: 86.2 us; the launch traced here: 85.7 us
  waiting for transfers between devices  43.6 us (51%)
  Pallas kernels  25.7 us (30%)
  starting transfers between devices  11.4 us (13%)
  other arithmetic  3.7 us (4%)
  local copies, waits for them, and re-layouts  1.06 us (1%)
    ppermute x1, waiting for transfers between devices, local(): from_upper = lax.ppermute(low, 'pairs', down)  35.8 us
    pallas_call x1, Pallas kernels, coupling_sums(): pl.pallas_call(term_kernel, grid_spec=pltpu.PrefetchScalarGridSpec(num_sc...  17 us
    ppermute x1, waiting for transfers between devices, local(): above = lax.ppermute(back, 'pairs', down)  6.09 us
    pallas_call x3, Pallas kernels, products(): pl.pallas_call(product_kernel, in_specs=[pl.BlockSpec(memory_space=pltpu....  4.1 us
    ppermute x1, starting transfers between devices, local(): below = lax.ppermute(blocks, 'pairs', up)  3.52 us
    ppermute x1, starting transfers between devices, local(): from_upper = lax.ppermute(low, 'pairs', down)  3.34 us
    pallas_call x1, Pallas kernels, last_sums(): pl.pallas_call(last_kernel, grid_spec=pltpu.PrefetchScalarGridSpec(num_sc...  2.7 us
    ppermute x1, starting transfers between devices, local(): from_lower = lax.ppermute(high, 'pairs', up)  2.08 us
  transfers between devices with their start and end apart: 7, of which 3 were waited for; matrix products, arithmetic and copies ran while one was open for 6% of the time, Pallas kernels for 27%

profile of v4, /device:TPU:12, one launch (start us, length us, event | category | flops | bytes accessed | tf_op | source)
XLA Modules:
  0.0 85.7 jit_solution(15172151566557300345)
XLA Ops:
  0.0 3.5 %collective-permute-start = (bf16[2,1024,256]{2,1,0:T(8,128)(2,1)}, bf16[2,1024,256]{2,1,0:T(8,128)(2,1)S(1)}, u32[]{:S(2)}, u32[]{:S(2)}) collective-permute-start(bf16[2,1024,256]{2,1,0:T(8,128)(2,1)} %left.2), channel_id=1, source_target_pairs={{0,2},{2,4},{4,6},{6,8},{8,10},{10,12},{12,14},{14,16},{16,18},{18... | collective-permute-start | bytes 3145736 | tf_op jit(solution)/shard_map/ppermute | solution.py:196
  3.5 0.1 constant_dynamic-slice_fusion.1
  3.6 0.1 copy.14
  3.7 0.8 constant_dynamic-slice_fusion
  4.5 0.1 copy.15.weights
  4.6 17.0 %coupling_sums.1 = (bf16[16,128,256]{2,1,0:T(8,128)(2,1)}, f32[16,128,256]{2,1,0:T(8,128)}, bf16[16,128,256]{2,1,0:T(8,128)(2,1)}) custom-call(s32[1]{0:T(128)} %bitcast.core, s32[16,4]{1,0:T(8,128)S(1)} %subtract_clamp_fusion.slots, f32[16,4]{1,0:T(8,128)S(1)} %copy.15.weights, bf16[16,4,256,256]{3,2,1,0:T(8,128)(2,1)} %margins.1, bf16[16,256,256]{2,1,0:T(8,128)(2,1)} %amps.3), custom_call_target="tpu_custom_call" | custom-call | flops 2147483648 | bytes 10485760 | tf_op jit(solution)/shard_map/coupling_sums/pallas_call | solution.py:41
  21.5 0.8 orbital_products.3
  22.3 0.1 collective-permute-start.1
  22.4 3.3 %collective-permute-start.4 = (bf16[16,128,256]{2,1,0:T(8,128)(2,1)}, bf16[16,128,256]{2,1,0:T(8,128)(2,1)S(1)}, u32[]{:S(2)}, u32[]{:S(2)}) collective-permute-start(bf16[16,128,256]{2,1,0:T(8,128)(2,1)} %get-tuple-element.30), channel_id=1, source_target_pairs={{2,0},{4,2},{6,4},{8,6},{10,8},{12,10},{14,12},{16,14},{18,16},{20... | collective-permute-start | bytes 3145736 | tf_op jit(solution)/shard_map/ppermute | solution.py:202
  25.8 0.9 %add.34 = f32[4,128,256]{2,1,0:T(8,128)} add(f32[4,128,256]{2,1,0:T(8,128)S(1)} %get-tuple-element.23, f32[4,128,256]{2,1,0:T(8,128)S(1)} %collective-permute-done.1) | non-fusion elementwise | flops 131072 | bytes 1572864 | tf_op jit(solution)/shard_map/add | solution.py:207
  26.7 1.8 %collective-permute-done.left.right = bf16[2,1024,256]{2,1,0:T(8,128)(2,1)S(1)} collective-permute-done((bf16[2,1024,256]{2,1,0:T(8,128)(2,1)}, bf16[2,1024,256]{2,1,0:T(8,128)(2,1)S(1)}, u32[]{:S(2)}, u32[]{:S(2)}) %collective-permute-start) | collective-permute-done | bytes 1048608 | tf_op jit(solution)/shard_map/ppermute | solution.py:196
  28.4 1.6 %orbital_products.5 = (f32[4,128,256]{2,1,0:T(8,128)S(1)}, f32[4,128,256]{2,1,0:T(8,128)}) custom-call(s32[1]{0:T(128)} %bitcast.core, bf16[2,1024,256]{2,1,0:T(8,128)(2,1)S(1)} %copy-done.1, bf16[2,1024,256]{2,1,0:T(8,128)(2,1)S(1)} %collective-permute-done.left.right), custom_call_target="tpu_custom_call" | custom-call | flops 1024 | bytes 1024 | tf_op jit(solution)/shard_map/orbital_products/pallas_call | solution.py:83
  30.1 1.6 %orbital_products.4 = (f32[4,128,256]{2,1,0:T(8,128)S(1)}, f32[4,128,256]{2,1,0:T(8,128)}) custom-call(s32[1]{0:T(128)} %bitcast.core, bf16[2,1024,256]{2,1,0:T(8,128)(2,1)S(1)} %collective-permute-done.left.right, bf16[2,1024,256]{2,1,0:T(8,128)(2,1)S(1)} %copy-done.1), custom_call_target="tpu_custom_call" | custom-call | flops 1024 | bytes 1024 | tf_op jit(solution)/shard_map/orbital_products/pallas_call | solution.py:83
  31.7 0.5 collective-permute-start.2
  32.2 2.1 %collective-permute-start.6 = (bf16[16,128,256]{2,1,0:T(8,128)(2,1)}, bf16[16,128,256]{2,1,0:T(8,128)(2,1)S(1)}, u32[]{:S(2)}, u32[]{:S(2)}) collective-permute-start(bf16[16,128,256]{2,1,0:T(8,128)(2,1)} %get-tuple-element.35), channel_id=1, source_target_pairs={{0,2},{2,4},{4,6},{6,8},{8,10},{10,12},{12,14},{14,16},{16,18},{18... | collective-permute-start | bytes 3145736 | tf_op jit(solution)/shard_map/ppermute | solution.py:203
  34.4 0.2 select_reduce_fusion
  34.6 1.3 %add.36 = f32[4,128,256]{2,1,0:T(8,128)S(1)} add(f32[4,128,256]{2,1,0:T(8,128)S(1)} %get-tuple-element.28, f32[4,128,256]{2,1,0:T(8,128)} %collective-permute-done.3) | non-fusion elementwise | flops 131072 | bytes 1572864 | tf_op jit(solution)/shard_map/add | solution.py:213
  35.9 1.3 %add_convert_fusion = bf16[4,128,256]{2,1,0:T(8,128)(2,1)S(1)} fusion(f32[4,128,256]{2,1,0:T(8,128)S(1)} %get-tuple-element.26, f32[4,128,256]{2,1,0:T(8,128)} %collective-permute-done.2), kind=kLoop, calls=%fused_computation.1 | loop fusion | flops 262144 | bytes 1310720 | tf_op jit(solution)/shard_map/convert_element_type | solution.py:211
  37.2 35.8 %collective-permute-done.4.high = bf16[16,128,256]{2,1,0:T(8,128)(2,1)S(1)} collective-permute-done((bf16[16,128,256]{2,1,0:T(8,128)(2,1)}, bf16[16,128,256]{2,1,0:T(8,128)(2,1)S(1)}, u32[]{:S(2)}, u32[]{:S(2)}) %collective-permute-start.4) | collective-permute-done | bytes 1048608 | tf_op jit(solution)/shard_map/ppermute | solution.py:202
  72.9 1.9 %collective-permute-start.5 = (bf16[4,128,256]{2,1,0:T(8,128)(2,1)S(1)}, bf16[4,128,256]{2,1,0:T(8,128)(2,1)S(1)}, u32[]{:S(2)}, u32[]{:S(2)}) collective-permute-start(bf16[4,128,256]{2,1,0:T(8,128)(2,1)S(1)} %add_convert_fusion), channel_id=1, source_target_pairs={{2,0},{4,2},{6,4},{8,6},{10,8},{12,10},{14,12},{16,14},{18,16},{20... | collective-permute-start | bytes 786440 | tf_op jit(solution)/shard_map/ppermute | solution.py:215
  74.9 0.1 pad_maximum_fusion.near
  75.0 1.9 %base_sums.1.base = f32[16,128,256]{2,1,0:T(8,128)S(1)} custom-call(s32[1]{0:T(128)} %bitcast.core, s32[16]{0:T(128)S(1)} %fusion.table, f32[16]{0:T(128)S(1)} %add.37.shift, f32[8,128,256]{2,1,0:T(8,128)S(1)} %pad_maximum_fusion.near, f32[16,1,256]{2,1,0:T(1,128)S(1)} %broadcast_in_dim.25.energy, bf16[16,256,256]{2,1,0:T(8,128)(2,1)S(1)} %copy-done.2, ...), custom_call_target="tpu_custom_call" | custom-call | flops 8192 | bytes 8192 | tf_op jit(solution)/shard_map/base_sums/pallas_call | solution.py:117
  76.9 6.1 %collective-permute-done.5.above = bf16[4,128,256]{2,1,0:T(8,128)(2,1)S(1)} collective-permute-done((bf16[4,128,256]{2,1,0:T(8,128)(2,1)S(1)}, bf16[4,128,256]{2,1,0:T(8,128)(2,1)S(1)}, u32[]{:S(2)}, u32[]{:S(2)}) %collective-permute-start.5) | collective-permute-done | bytes 262176 | tf_op jit(solution)/shard_map/ppermute | solution.py:215
  83.0 2.7 %last_sums.1 = f32[16,128,256]{2,1,0:T(8,128)} custom-call(s32[1]{0:T(128)} %bitcast.core, s32[16]{0:T(128)S(1)} %fusion.table, s32[16]{0:T(128)S(1)} %copy-done.4, bf16[4,128,256]{2,1,0:T(8,128)(2,1)S(1)} %collective-permute-done.5.above, f32[16,128,256]{2,1,0:T(8,128)S(1)} %base_sums.1.base, bf16[16,128,256]{2,1,0:T(8,128)(2,1)S(1)} %collective-permute-done.6.low, ...), custom_call_target="tpu_custom_call" | custom-call | flops 3145728 | bytes 6291456 | tf_op jit(solution)/shard_map/last_sums/pallas_call | solution.py:157
  (28 shorter events, 0.1 us)
Async XLA Ops:
  0.0 3.5 %copy-start = (s32[256,4]{0,1:T(4,128)S(1)}, s32[256,4]{0,1:T(4,128)}, u32[]{:S(2)}) copy-start(s32[256,4]{0,1:T(4,128)} %param.14) | copy-start | bytes 12292
  0.0 28.4 %collective-permute-start = (bf16[2,1024,256]{2,1,0:T(8,128)(2,1)}, bf16[2,1024,256]{2,1,0:T(8,128)(2,1)S(1)}, u32[]{:S(2)}, u32[]{:S(2)}) collective-permute-start(bf16[2,1024,256]{2,1,0:T(8,128)(2,1)} %left.2), channel_id=1, source_target_pairs={{0,2},{2,4},{4,6},{6,8},{8,10},{10,12},{12,14},{14,16},{16,18},{18... | collective-permute-start | bytes 3145736 | tf_op jit(solution)/shard_map/ppermute | solution.py:196
  4.6 17.0 %copy-start.1 = (bf16[2,1024,256]{2,1,0:T(8,128)(2,1)S(1)}, bf16[2,1024,256]{2,1,0:T(8,128)(2,1)}, u32[]{:S(2)}) copy-start(bf16[2,1024,256]{2,1,0:T(8,128)(2,1)} %left.2) | copy-start | bytes 3145732
  22.3 3.4 %collective-permute-start.1 = (f32[4,128,256]{2,1,0:T(8,128)S(1)}, f32[4,128,256]{2,1,0:T(8,128)S(1)}, u32[]{:S(2)}, u32[]{:S(2)}) collective-permute-start(f32[4,128,256]{2,1,0:T(8,128)S(1)} %get-tuple-element.24), channel_id=1, source_target_pairs={{0,1},{1,0},{2,3},{3,2},{4,5},{5,4},{6,7},{7,6},{8,9},{9,8},{10,11... | collective-permute-start | bytes 1572872 | tf_op jit(solution)/shard_map/ppermute | solution.py:207
  22.4 50.5 %collective-permute-start.4 = (bf16[16,128,256]{2,1,0:T(8,128)(2,1)}, bf16[16,128,256]{2,1,0:T(8,128)(2,1)S(1)}, u32[]{:S(2)}, u32[]{:S(2)}) collective-permute-start(bf16[16,128,256]{2,1,0:T(8,128)(2,1)} %get-tuple-element.30), channel_id=1, source_target_pairs={{2,0},{4,2},{6,4},{8,6},{10,8},{12,10},{14,12},{16,14},{18,16},{20... | collective-permute-start | bytes 3145736 | tf_op jit(solution)/shard_map/ppermute | solution.py:202
  26.7 7.7 %copy-start.6 = (f32[16,256]{1,0:T(8,128)S(1)}, f32[16,256]{1,0:T(8,128)}, u32[]{:S(2)}) copy-start(f32[16,256]{1,0:T(8,128)} %param.16) | copy-start | bytes 49156
  26.7 7.7 %copy-start.7 = (s32[16,2]{0,1:T(2,128)S(1)}, s32[16,2]{0,1:T(2,128)}, u32[]{:S(2)}) copy-start(s32[16,2]{0,1:T(2,128)} %param.10) | copy-start | bytes 388
  26.7 7.7 %copy-start.8 = (f32[32]{0:T(128)S(1)}, f32[32]{0:T(128)}, u32[]{:S(2)}) copy-start(f32[32]{0:T(128)} %param.17) | copy-start | bytes 388
  30.1 4.5 %collective-permute-start.3 = (f32[4,128,256]{2,1,0:T(8,128)}, f32[4,128,256]{2,1,0:T(8,128)}, u32[]{:S(2)}, u32[]{:S(2)}) collective-permute-start(f32[4,128,256]{2,1,0:T(8,128)} %get-tuple-element.29), channel_id=1, source_target_pairs={{0,1},{1,0},{2,3},{3,2},{4,5},{5,4},{6,7},{7,6},{8,9},{9,8},{10,11... | collective-permute-start | bytes 1572872 | tf_op jit(solution)/shard_map/ppermute | solution.py:213
  31.7 4.2 %collective-permute-start.2 = (f32[4,128,256]{2,1,0:T(8,128)}, f32[4,128,256]{2,1,0:T(8,128)}, u32[]{:S(2)}, u32[]{:S(2)}) collective-permute-start(f32[4,128,256]{2,1,0:T(8,128)} %get-tuple-element.27), channel_id=1, source_target_pairs={{0,1},{1,0},{2,3},{3,2},{4,5},{5,4},{6,7},{7,6},{8,9},{9,8},{10,11... | collective-permute-start | bytes 1572872 | tf_op jit(solution)/shard_map/ppermute | solution.py:211
  32.2 44.7 %collective-permute-start.6 = (bf16[16,128,256]{2,1,0:T(8,128)(2,1)}, bf16[16,128,256]{2,1,0:T(8,128)(2,1)S(1)}, u32[]{:S(2)}, u32[]{:S(2)}) collective-permute-start(bf16[16,128,256]{2,1,0:T(8,128)(2,1)} %get-tuple-element.35), channel_id=1, source_target_pairs={{0,2},{2,4},{4,6},{6,8},{8,10},{10,12},{12,14},{14,16},{16,18},{18... | collective-permute-start | bytes 3145736 | tf_op jit(solution)/shard_map/ppermute | solution.py:203
  34.3 40.5 %copy-start.5 = (f32[4,128,256]{2,1,0:T(8,128)S(1)}, f32[4,128,256]{2,1,0:T(8,128)}, u32[]{:S(2)}) copy-start(f32[4,128,256]{2,1,0:T(8,128)} %add.34) | copy-start | bytes 1572868
  34.6 40.4 %copy-start.3 = (f32[16,128,256]{2,1,0:T(8,128)S(1)}, f32[16,128,256]{2,1,0:T(8,128)}, u32[]{:S(2)}) copy-start(f32[16,128,256]{2,1,0:T(8,128)} %get-tuple-element.34.mid) | copy-start | bytes 6291460
  35.9 39.1 %copy-start.2 = (bf16[16,256,256]{2,1,0:T(8,128)(2,1)S(1)}, bf16[16,256,256]{2,1,0:T(8,128)(2,1)}, u32[]{:S(2)}) copy-start(bf16[16,256,256]{2,1,0:T(8,128)(2,1)} %amps.3) | copy-start | bytes 6291460
  72.9 10.1 %collective-permute-start.5 = (bf16[4,128,256]{2,1,0:T(8,128)(2,1)S(1)}, bf16[4,128,256]{2,1,0:T(8,128)(2,1)S(1)}, u32[]{:S(2)}, u32[]{:S(2)}) collective-permute-start(bf16[4,128,256]{2,1,0:T(8,128)(2,1)S(1)} %add_convert_fusion), channel_id=1, source_target_pairs={{2,0},{4,2},{6,4},{8,6},{10,8},{12,10},{14,12},{16,14},{18,16},{20... | collective-permute-start | bytes 786440 | tf_op jit(solution)/shard_map/ppermute | solution.py:215
  75.0 8.0 %copy-start.4 = (s32[16]{0:T(128)S(1)}, s32[16]{0:T(128)}, u32[]{:S(2)}) copy-start(s32[16]{0:T(128)} %counts.1) | copy-start | bytes 196
